TPU v7x, 32 devices: a whole 2x2x4 slice. The times are simulated.
32 devices in a mesh: row: 8 (over z, x), col: 4 (over y, core).
Axes of the slice: x: 2, y: 2, z: 4, core: 2. Of those that a mesh axis runs over, the one named last changes fastest.
Arguments:
- panel: bfloat16 [1024, 18432], P('col', 'row'), may hold values from -6 to 6
- mask: int32 [1024], P('row'), may hold values 0 or 1
- timesteps: int32 [1], replicated, may hold values from 3 to 31
- cot_gate: bfloat16 [1024, 36864], P('row', 'col'), may hold values from -6 to 6
Outputs:
- grad_gate: float32 [18432, 36864], P('row', 'col')
All inputs are finite; a program needn't handle non-finite values. No bound on the sum of `mask` on one device may be relied on, other than what follows from the above.
Results may differ from a plain program's by a relative error of at most 0.0027.
Values may be sent and summed in bfloat16 or wider, within the bound.
No kernel may reach another device: no remote copies, remote signals or barrier semaphores. Data moves between devices by JAX's collectives and lax.ppermute only.
A program may use at most 256 MiB of HBM per device.

v0:
```python
import math

import jax
import jax.numpy as jnp
from jax import lax
from jax.sharding import PartitionSpec as P

STEPS = 32


def token_weights(mask, timesteps, first, seq_len, total):
    count = mask.shape[0]
    position = first + jnp.arange(count, dtype=jnp.int32)
    which = position // seq_len
    onehot = which[:, None] == jnp.arange(timesteps.shape[0], dtype=jnp.int32)[None, :]
    level = jnp.sum(jnp.where(onehot, timesteps[None, :], 0), axis=1)
    scale = 1.0 / math.sqrt(total)
    return mask.astype(jnp.float32) * (STEPS / (level + 1).astype(jnp.float32)) * scale


def body(panel, mask, timesteps, cot_gate):
    tok_rows = cot_gate.shape[0]
    total = tok_rows * lax.axis_size("row")
    seq_len = total // timesteps.shape[0]
    first = lax.axis_index("row") * tok_rows
    weights = token_weights(mask, timesteps, first, seq_len, total)
    weighted = (cot_gate.astype(jnp.float32) * weights[:, None]).astype(jnp.bfloat16)
    whole_panel = lax.all_gather(panel, "col", axis=0, tiled=True)
    dims = (((0,), (0,)), ((), ()))
    whole_cot = lax.all_gather(weighted, "row", axis=0, tiled=True)
    grad_gate = lax.dot_general(whole_panel, whole_cot, dims, preferred_element_type=jnp.float32)
    return grad_gate


def solution(mesh):
    placed = (P("col", "row"), P("row"), P(), P("row", "col"))
    return jax.shard_map(
        body, mesh=mesh, in_specs=placed, out_specs=P("row", "col"), check_vma=False
    )
```

profile of v0, /device:TPU:0, one launch (start us, length us, event | category | flops | bytes accessed | tf_op | source)
XLA Modules:
  0.0 555.1 jit_solution(7775165507917505064)
XLA Ops:
  6.5 0.0 all-gather.5.cloned.1.call-start
  6.5 0.7 all-gather.5.cloned.1.call-update
  7.3 0.0 all-gather.3.cloned.1.call-start
  8.0 0.7 fusion.2
  8.6 3.6 multiply_convert_fusion
  12.2 0.0 all-gather.3.cloned.1.call-update
  12.2 36.9 %all-gather.5.cloned.1.call-done = bf16[1024,2304]{1,0:T(8,128)(2,1)} async-done(((bf16[256,2304]{1,0:T(8,128)(2,1)}), bf16[1024,2304]{1,0:T(8,128)(2,1)}) %all-gather.5.cloned.1.call-update) | async-done | bytes 4718608 | tf_op jit(solution)/shard_map/all_gather | solution.py:28
  49.1 364.0 %all-gather.3.cloned.1.call-done = bf16[1024,9216]{1,0:T(8,128)(2,1)} async-done(((bf16[128,9216]{1,0:T(8,128)(2,1)}), bf16[1024,9216]{1,0:T(8,128)(2,1)}) %all-gather.3.cloned.1.call-update) | async-done | bytes 18874384 | tf_op jit(solution)/shard_map/all_gather | solution.py:30
  413.1 53.0 %convolution_bitcast_fusion = f32[2304,9216]{0,1:T(8,128)} fusion(bf16[1024,9216]{1,0:T(8,128)(2,1)} %all-gather.3.cloned.1.call-done, bf16[1024,2304]{1,0:T(8,128)(2,1)} %all-gather.5.cloned.1.call-done), kind=kOutput, calls=%fused_computation | convolution fusion | flops 43486543872 | bytes 108527616 | tf_op jit(solution)/shard_map/dot_general | solution.py:31
  466.2 82.1 %copy.5 = f32[2304,9216]{1,0:T(8,128)} copy(f32[2304,9216]{0,1:T(8,128)} %convolution_bitcast_fusion) | data formatting | bytes 169869312 | tf_op jit(solution)/shard_map/dot_general | solution.py:31
Async XLA Ops:
  6.5 42.6 %all-gather.5.cloned.1.call-start = ((), (), s32[]{:S(2)}) async-start(), calls=%async_computation.1 | async-start | bytes 5898240 | tf_op jit(solution)/shard_map/all_gather | solution.py:28
  7.3 405.9 %all-gather.3.cloned.1.call-start = ((), (), s32[]{:S(2)}) async-start(), calls=%async_computation | async-start | bytes 21233664 | tf_op jit(solution)/shard_map/all_gather | solution.py:30
Sparse Core Ops, SparseCore 0:
  8.9 40.1 all-gather.4
  50.6 362.4 all-gather.2
where the time goes:
time: 556 us; the launch traced here: 555 us
  waiting for transfers between devices  402 us (72%)
  local copies, waits for them, and re-layouts  82.1 us (15%)
  matrix products  53 us (10%)
  between operations  14.1 us (3%)
    all_gather x1, waiting for transfers between devices, body(): whole_cot = lax.all_gather(weighted, 'row', axis=0, tiled=True)  364 us
    dot_general x1, local copies, waits for them, and re-layouts, body(): lax.dot_general(whole_panel, whole_cot, dims, preferred_element_type=jnp....  82.1 us
    dot_general x1, matrix products, body(): lax.dot_general(whole_panel, whole_cot, dims, preferred_element_type=jnp....  53 us
    all_gather x1, waiting for transfers between devices, body(): whole_panel = lax.all_gather(panel, 'col', axis=0, tiled=True)  36.9 us
  transfers between devices with their start and end apart: 2, of which 2 were waited for; matrix products, arithmetic and copies ran while one was open for 1% of the time, Pallas kernels for 0%

commit v1 on v0

v1 whole, which is shorter than its diff:
```python
import functools
import math

import jax
import jax.numpy as jnp
import numpy as np
from jax import lax
from jax.experimental import pallas as pl
from jax.experimental.pallas import tpu as pltpu
from jax.sharding import PartitionSpec as P

STEPS = 32
LANES = 128
ROWS = 80
SPLIT = (2, 4)
TIGHT = True
STAGGER = 3
LIMIT = 28 * 2**20


def token_weights(mask, timesteps, first, seq_len, total):
    count = mask.shape[0]
    position = first + jnp.arange(count, dtype=jnp.int32)
    which = position // seq_len
    onehot = which[:, None] == jnp.arange(timesteps.shape[0], dtype=jnp.int32)[None, :]
    level = jnp.sum(jnp.where(onehot, timesteps[None, :], 0), axis=1)
    scale = 1.0 / math.sqrt(total)
    return mask.astype(jnp.float32) * (STEPS / (level + 1).astype(jnp.float32)) * scale


def cycle(n):
    fast = 1
    while fast * fast * 4 <= n:
        fast *= 2
    slow = n // fast
    walk = [z * fast for z in range(slow)]
    for i, z in enumerate(reversed(range(slow))):
        xs = range(1, fast) if i % 2 == 0 else reversed(range(1, fast))
        walk += [z * fast + x for x in xs]
    return walk


def chunks_of(width, split):
    tiles = width // LANES
    fore = (tiles + 1) // 2
    out = []
    for first, count in ((0, fore), (fore, tiles - fore)):
        if tiles % 2 or count % sum(split):
            split = (1,)
        ranges, at = [], first
        for part in split:
            size = part * (count // sum(split))
            ranges.append((at * LANES, size * LANES))
            at += size
        out.append(ranges)
    return out


def tile_of(first, width, most):
    best = LANES
    for size in range(LANES, most + 1, LANES):
        if first % size == 0 and width % size == 0:
            best = size
    return best


def picker(mask_row, base, rows):
    count = mask_row.shape[1]
    kept = jnp.broadcast_to(mask_row, (8, count)).astype(jnp.float32)
    before = lax.broadcasted_iota(jnp.int32, (count, count), 0)
    after = lax.broadcasted_iota(jnp.int32, (count, count), 1)
    upper = jnp.where(before <= after, 1.0, 0.0)
    rank = jnp.dot(kept.astype(jnp.bfloat16), upper.astype(jnp.bfloat16), preferred_element_type=jnp.float32)
    rank = jnp.where(kept > 0, rank, 0.0)[0:1]
    place = lax.broadcasted_iota(jnp.int32, (rows, count), 0) + (base + 1)
    return jnp.where(place.astype(jnp.float32) == rank, 1.0, 0.0).astype(jnp.bfloat16)


def pack_kernel(base, rows, unit, ranges, mask_ref, weight_ref, cot_ref, *outs):
    count = cot_ref.shape[0]
    pick = picker(mask_ref[...], base, rows)
    across = lax.broadcasted_iota(jnp.int32, (count, count), 0)
    along = lax.broadcasted_iota(jnp.int32, (count, count), 1)
    weight = jnp.sum(jnp.where(across == along, weight_ref[...], 0.0), axis=1, keepdims=True)
    weighted = (cot_ref[...].astype(jnp.float32) * weight).astype(jnp.bfloat16)
    packed = jnp.dot(pick, weighted, preferred_element_type=jnp.float32).astype(jnp.bfloat16)
    steps = [width // unit for _, width in ranges]
    for k, out in enumerate(outs):
        for u in range(steps[k]):

            @pl.when(pl.program_id(0) == sum(steps[:k]) + u)
            def _(out=out, u=u):
                out[:, u * unit : (u + 1) * unit] = packed


def pack(cot, mask, weights, base, rows, ranges):
    count = cot.shape[0]
    unit = functools.reduce(math.gcd, [v for r in ranges for v in r if v])
    (first, width), (second, other) = ranges
    steps = width // unit
    return pl.pallas_call(
        functools.partial(pack_kernel, base, rows, unit, ranges),
        grid=((width + other) // unit,),
        in_specs=[
            pl.BlockSpec((1, count), lambda i: (0, 0)),
            pl.BlockSpec((1, count), lambda i: (0, 0)),
            pl.BlockSpec(
                (count, unit),
                lambda i: (0, jnp.where(i < steps, first // unit + i, second // unit + i - steps)),
            ),
        ],
        out_specs=[pl.BlockSpec((rows, w), lambda i: (0, 0)) for _, w in ranges],
        out_shape=[jax.ShapeDtypeStruct((rows, w), jnp.bfloat16) for _, w in ranges],
        compiler_params=pltpu.CompilerParams(vmem_limit_bytes=LIMIT),
    )(mask[None, :], weights[None, :], cot)


def select_kernel(base, rows, plan_ref, masks_ref, *refs):
    parts, (out_ref, most_ref) = refs[:-2], refs[-2:]
    kept = jnp.sum(masks_ref[...].astype(jnp.float32), axis=1, keepdims=True)
    most_ref[...] = jnp.broadcast_to(jnp.max(kept, axis=0, keepdims=True), most_ref.shape)
    per = masks_ref.shape[1]
    got, at = [], 0
    for part in parts:
        for b in range(part.shape[0] // per):
            pick = picker(masks_ref[pl.ds(plan_ref[2 * plan_ref.shape[0] // 3 + at], 1), :], base, rows)
            block = part[b * per : (b + 1) * per, :]
            got.append(jnp.dot(pick, block, preferred_element_type=jnp.float32))
            at += 1
    out_ref[...] = jnp.concatenate(got, axis=0).T.astype(jnp.bfloat16)


def select(parts, masks, plan, base, rows):
    features = parts[0].shape[1]
    tile = tile_of(0, features, 384)
    if features % tile:
        tile = features
    owners = masks.shape[0]
    return pl.pallas_call(
        functools.partial(select_kernel, base, rows),
        grid_spec=pltpu.PrefetchScalarGridSpec(
            num_scalar_prefetch=1,
            grid=(features // tile,),
            in_specs=[pl.BlockSpec(masks.shape, lambda i, plan: (0, 0))]
            + [pl.BlockSpec((p.shape[0], tile), lambda i, plan: (0, i)) for p in parts],
            out_specs=[
                pl.BlockSpec((tile, owners * rows), lambda i, plan: (i, 0)),
                pl.BlockSpec((8, LANES), lambda i, plan: (0, 0)),
            ],
        ),
        out_shape=[
            jax.ShapeDtypeStruct((features, owners * rows), jnp.bfloat16),
            jax.ShapeDtypeStruct((8, LANES), jnp.float32),
        ],
        compiler_params=pltpu.CompilerParams(vmem_limit_bytes=LIMIT),
    )(plan, masks, *parts)


def join_kernel(one_ref, two_ref, out_ref):
    out_ref[...] = jnp.concatenate([one_ref[...], two_ref[...]], axis=0)


def join(one, two):
    return pl.pallas_call(
        join_kernel,
        out_shape=jax.ShapeDtypeStruct((2 * one.shape[0], one.shape[1]), one.dtype),
        compiler_params=pltpu.CompilerParams(vmem_limit_bytes=2**20),
    )(one, two)


def product_kernel(n, cap, rows, adds, line, plan_ref, most_ref, panel_ref, *refs):
    pieces, (out_ref, mark_ref, depth_ref) = refs[:n], refs[-3:]
    i = pl.program_id(1)
    mark_ref[...] = most_ref[...]

    @pl.when(i == 0)
    def _():
        for j in range(n):
            depth_ref[pl.ds(pl.multiple_of(plan_ref[line * n + j] * cap, 16), cap), :] = pieces[j][...]

    panel = panel_ref[pl.ds(pl.multiple_of(i * rows, 16), rows), :]
    result = jnp.dot(panel, depth_ref[...], preferred_element_type=jnp.float32)
    if adds:
        result = result + refs[n][...]
    out_ref[...] = result


def product(panel_t, most, pieces, plan, line, out, adds, first, shape):
    n, (cap, width) = len(pieces), pieces[0].shape
    features, depth = panel_t.shape
    blocks = 3 if features % (3 * 16) == 0 else 1
    rows = features // blocks
    tile = tile_of(first, width, 768 if adds else 1536)
    place = lambda j, i, plan: (i, first // tile + j)
    specs = [
        pl.BlockSpec((8, LANES), lambda j, i, plan: (0, 0)),
        pl.BlockSpec((features, depth), lambda j, i, plan: (0, 0)),
    ]
    specs += [pl.BlockSpec((cap, tile), lambda j, i, plan: (0, j)) for _ in pieces]
    args = [plan, most, panel_t, *pieces]
    aliases = {}
    if out is not None:
        specs.append(pl.BlockSpec((rows, tile), place) if adds else pl.BlockSpec(memory_space=pl.ANY))
        args.append(out)
        aliases = {len(args) - 1: 0}
    return pl.pallas_call(
        functools.partial(product_kernel, n, cap, rows, adds, line),
        grid_spec=pltpu.PrefetchScalarGridSpec(
            num_scalar_prefetch=1,
            grid=(width // tile, blocks),
            in_specs=specs,
            out_specs=[
                pl.BlockSpec((rows, tile), place),
                pl.BlockSpec((8, LANES), lambda j, i, plan: (0, 0)),
            ],
            scratch_shapes=[pltpu.VMEM((depth, tile), jnp.bfloat16)],
        ),
        out_shape=[
            jax.ShapeDtypeStruct(shape, jnp.float32),
            jax.ShapeDtypeStruct((8, LANES), jnp.float32),
        ],
        input_output_aliases=aliases,
        compiler_params=pltpu.CompilerParams(vmem_limit_bytes=LIMIT),
        cost_estimate=pl.CostEstimate(
            flops=2 * features * depth * width,
            bytes_accessed=features * (4 * width + 2 * depth) + 2 * depth * width,
            transcendentals=0,
        ),
    )(*args)


def after(value, *earlier):
    return lax.optimization_barrier((value, *earlier))[0]


def plans(n, cols, several):
    walk = cycle(n)
    table = np.zeros((n, cols, 3, n), np.int32)
    for me in range(n):
        for col in range(cols):
            turn = col if cols == 4 else 0
            place = walk.index(me)
            for s in range(n):
                for line, owner in enumerate((walk[(place - s) % n], walk[(place + s) % n])):
                    table[me, col, line, s] = ((owner // several) ^ turn) * several + owner % several
                table[me, col, 2, s] = (((s // several) ^ turn) * several + s % several) ^ me
    return jnp.asarray(table.reshape(n * cols, 3 * n))


def body(panel, mask, timesteps, cot_gate):
    n, cols = lax.axis_size("row"), lax.axis_size("col")
    me, col = lax.axis_index("row"), lax.axis_index("col")
    per, width = cot_gate.shape
    shape = (panel.shape[1], width)
    total = per * n
    weights = token_weights(mask, timesteps, me * per, total // timesteps.shape[0], total)
    walk = cycle(n)
    fore = [(walk[i], walk[(i + 1) % n]) for i in range(n)]
    back = [(b, a) for a, b in fore]

    several = panel.shape[0] // per
    plan = lax.dynamic_slice(plans(n, cols, several), (me * cols + col, 0), (1, 3 * n))[0]
    cot_gate = after(cot_gate, plan)

    def swap(value, axis, size, bit):
        return lax.ppermute(value, axis, [(i, i ^ bit) for i in range(size)])

    cap = min(ROWS, per)
    spans = chunks_of(width, SPLIT)
    chunks = len(spans[0])
    packed = [pack(cot_gate, mask, weights, 0, cap, (spans[0][k], spans[1][k])) for k in range(chunks)]
    rings = [[[fore_piece], [back_piece]] for fore_piece, back_piece in packed]
    out, masks, panel_t = None, mask[None, :], None
    parts = [panel]
    bit, before, marks = 1, [packed[0][0]], []
    last = (chunks - 1) * STAGGER + n + 1
    for r in range(1, last + 1):
        fresh = []
        for k in range(chunks):
            step = r - STAGGER * k
            if 1 <= step < n:
                for ring, perm in zip(rings[k], (fore, back)):
                    tied = marks + (before if TIGHT or step == 1 else [])
                    ring.append(lax.ppermute(after(ring[-1], *tied), "row", perm))
                    fresh.append(ring[-1])
        if bit < n:
            masks = join(masks, swap(after(masks, *before), "row", n, bit))
            fresh.append(masks)
            bit *= 2
        if r == 1 and cols == 4:
            parts.append(swap(after(panel, *before), "col", cols, 1))
            parts.append(swap(after(panel, *before), "col", cols, 2))
        elif r == 1:
            parts = [lax.all_gather(panel, "col", axis=0, tiled=True)]
        if r == max(n - 4, 2) and cols == 4:
            parts.append(swap(after(parts[2], *before), "col", cols, 1))
        marks = []
        if r == n - 2:
            panel_t, most = select(parts, after(masks, *before), plan, 0, cap)
            marks = [most]
        for k in range(chunks):
            side = r - STAGGER * k - n
            if 0 <= side < 2:
                pieces = rings[k][side]
                pieces = [after(pieces[0], *before), *pieces[1:]]
                out, most = product(panel_t, most, pieces, plan, side, out, False, spans[side][k][0], shape)
                marks.append(most)
        before = fresh or before
    if cap == per:
        return out

    def rest(i, out):
        cot, near, weight, *panels = lax.optimization_barrier((cot_gate, mask, weights, *parts, masks, i))[:-1]
        spans = chunks_of(width, (1,))
        left = pack(cot, near, weight, cap, per - cap, (spans[0][0], spans[1][0]))
        panel_t, mark = select(panels[:-1], panels[-1], plan, cap, per - cap)
        for piece, perm, line, span in zip(left, (fore, back), (0, 1), spans):
            pieces = [piece]
            for _ in range(n - 1):
                pieces.append(lax.ppermute(pieces[-1], "row", perm))
            out, mark = product(panel_t, mark, pieces, plan, line, out, True, span[0][0], shape)
        return out

    return lax.fori_loop(0, (most[0, 0] > cap).astype(jnp.int32), rest, out)


def solution(mesh):
    placed = (P("col", "row"), P("row"), P(), P("row", "col"))
    return jax.shard_map(
        body, mesh=mesh, in_specs=placed, out_specs=P("row", "col"), check_vma=False
    )
```

time: 556 us -> 168 us (0.30)
  waiting for transfers between devices: 402 us -> 61.8 us
  local copies, waits for them, and re-layouts: 82.1 us -> 1.29 us
  Pallas kernels: 0 us -> 65.4 us
  matrix products: 53 us -> 0 us
  starting transfers between devices: 0.04 us -> 36.7 us
  between operations: 14.1 us -> 1.6 us
    all_gather x2 -> x0, waiting for transfers between devices: 401 us -> none  [the longest x1 364 us: body(): whole_cot = lax.all_gather(weighted, 'row', axis=0, tiled=True)]
    dot_general x1 -> x0, local copies, waits for them, and re-layouts: 82.1 us -> none  [body(): lax.dot_general(whole_panel, whole_cot, dims, preferred_element_type=jnp....]
    pallas_call x0 -> x10, Pallas kernels: none -> 65.4 us  [the longest x4 49.6 us: product(): pl.pallas_call(functools.partial(product_kernel, n, cap, rows, adds, line...]
    ppermute x0 -> x34, waiting for transfers between devices: none -> 61.8 us  [the longest x28 51.2 us: body(): ring.append(lax.ppermute(after(ring[-1], *tied), 'row', perm))]
    dot_general x1 -> x0, matrix products: 53 us -> none  [body(): lax.dot_general(whole_panel, whole_cot, dims, preferred_element_type=jnp....]
    ppermute x0 -> x34, starting transfers between devices: none -> 36.7 us  [the longest x28 27.3 us: body(): ring.append(lax.ppermute(after(ring[-1], *tied), 'row', perm))]
  transfers between devices with their start and end apart: 2 -> 34, of which waited for: 2 -> 14; matrix products, arithmetic and copies ran while one was open for 1% -> 0% of each run, Pallas kernels for 0% -> 19%
where the time goes in v1:
time: 168 us
  Pallas kernels  65.4 us (39%)
  waiting for transfers between devices  61.8 us (37%)
  starting transfers between devices  36.7 us (22%)
    ppermute x28, waiting for transfers between devices, body(): ring.append(lax.ppermute(after(ring[-1], *tied), 'row', perm))  51.2 us
    pallas_call x4, Pallas kernels, product(): pl.pallas_call(functools.partial(product_kernel, n, cap, rows, adds, line...  49.6 us
    ppermute x28, starting transfers between devices, body(): ring.append(lax.ppermute(after(ring[-1], *tied), 'row', perm))  27.3 us
    ppermute x6, waiting for transfers between devices, swap(): return lax.ppermute(value, axis, [(i, i ^ bit) for i in range(size)])  10.6 us
    pallas_call x1, Pallas kernels, select(): pl.pallas_call(functools.partial(select_kernel, base, rows), grid_spec=pl...  10.2 us
    ppermute x6, starting transfers between devices, swap(): return lax.ppermute(value, axis, [(i, i ^ bit) for i in range(size)])  9.39 us
    pallas_call x2, Pallas kernels, pack(): pl.pallas_call(functools.partial(pack_kernel, base, rows, unit, ranges),...  4.95 us
  transfers between devices with their start and end apart: 34, of which 14 were waited for; matrix products, arithmetic and copies ran while one was open for 0% of the time, Pallas kernels for 19%

profile of v1, /device:TPU:0, one launch (start us, length us, event | category | flops | bytes accessed | tf_op | source)
XLA Modules:
  0.0 167.7 jit_solution(15987046112670594879)
XLA Ops:
  0.7 0.7 dynamic-slice_bitcast_fusion.plan_ref
  1.4 0.7 fusion.3.weight_ref
  2.0 1.8 %shard_map.55 = (bf16[80,1536]{1,0:T(8,128)(2,1)S(1)}, bf16[80,1536]{1,0:T(8,128)(2,1)S(1)}) custom-call(s32[1,128]{1,0:T(1,128)} %bitcast.15, f32[1,128]{1,0:T(1,128)S(1)} %fusion.3.weight_ref, bf16[128,9216]{1,0:T(8,128)(2,1)} %cot_ref.1), custom_call_target="tpu_custom_call" | custom-call | tf_op jit(solution)/shard_map/pallas_call | solution.py:101
  3.8 3.0 %collective-permute-start.32 = (bf16[256,2304]{1,0:T(8,128)(2,1)}, bf16[256,2304]{1,0:T(8,128)(2,1)S(1)}, u32[]{:S(2)}, u32[]{:S(2)}) collective-permute-start(bf16[256,2304]{1,0:T(8,128)(2,1)} %refs_0_.1), channel_id=1, source_target_pairs={{0,2},{1,3},{2,0},{3,1},{4,6},{5,7},{6,4},{7,5},{8,10},{9,11},{10,... | collective-permute-start | bytes 3538952 | tf_op jit(solution)/shard_map/ppermute | solution.py:266
  6.9 1.6 collective-permute-start.15
  8.9 1.5 collective-permute-start.14
  10.4 4.0 %collective-permute-done.14.two_ref = s32[1,128]{1,0:T(1,128)S(1)} collective-permute-done((s32[1,128]{1,0:T(1,128)}, s32[1,128]{1,0:T(1,128)S(1)}, u32[]{:S(2)}, u32[]{:S(2)}) %collective-permute-start.14) | collective-permute-done | bytes 544 | tf_op jit(solution)/shard_map/ppermute | solution.py:266
  14.3 0.7 shard_map.56.one_ref
  15.0 0.6 collective-permute-done.16.refs_1_
  15.6 1.6 collective-permute-start.18
  17.6 1.6 collective-permute-start.17
  19.2 4.2 %collective-permute-done.17.two_ref = s32[2,128]{1,0:T(2,128)S(1)} collective-permute-done((s32[2,128]{1,0:T(2,128)S(1)}, s32[2,128]{1,0:T(2,128)S(1)}, u32[]{:S(2)}, u32[]{:S(2)}) %collective-permute-start.17) | collective-permute-done | bytes 1056 | tf_op jit(solution)/shard_map/ppermute | solution.py:266
  23.4 1.8 %collective-permute-start.21 = (bf16[80,1536]{1,0:T(8,128)(2,1)S(1)}, bf16[80,1536]{1,0:T(8,128)(2,1)S(1)}, u32[]{:S(2)}, u32[]{:S(2)}) collective-permute-start(bf16[80,1536]{1,0:T(8,128)(2,1)S(1)} %collective-permute-done.18.refs_2_), channel_id=1, source_target_pairs={{0,8},{8,16},{16,24},{24,28},{28,20},{20,12},{12,4},{4,0},{1,9},{9... | collective-permute-start | bytes 737288 | tf_op jit(solution)/shard_map/ppermute | solution.py:284
  25.5 3.3 %collective-permute-start.20 = (s32[4,128]{1,0:T(4,128)S(1)}, s32[4,128]{1,0:T(4,128)S(1)}, u32[]{:S(2)}, u32[]{:S(2)}) collective-permute-start(s32[4,128]{1,0:T(4,128)S(1)} %shard_map.57.one_ref), channel_id=1, source_target_pairs={{0,16},{4,20},{8,24},{12,28},{16,0},{20,4},{24,8},{28,12},{1,17},{... | collective-permute-start | bytes 6152 | tf_op jit(solution)/shard_map/ppermute | solution.py:266
  28.8 3.2 %shard_map.59 = (bf16[80,3072]{1,0:T(8,128)(2,1)S(1)}, bf16[80,3072]{1,0:T(8,128)(2,1)S(1)}) custom-call(s32[1,128]{1,0:T(1,128)} %bitcast.18, f32[1,128]{1,0:T(1,128)S(1)} %fusion.3.weight_ref, bf16[128,9216]{1,0:T(8,128)(2,1)} %cot_ref.1), custom_call_target="tpu_custom_call" | custom-call | tf_op jit(solution)/shard_map/pallas_call | solution.py:101
  32.0 2.4 %collective-permute-done.20.two_ref = s32[4,128]{1,0:T(4,128)S(1)} collective-permute-done((s32[4,128]{1,0:T(4,128)S(1)}, s32[4,128]{1,0:T(4,128)S(1)}, u32[]{:S(2)}, u32[]{:S(2)}) %collective-permute-start.20) | collective-permute-done | bytes 2080 | tf_op jit(solution)/shard_map/ppermute | solution.py:266
  34.5 2.0 %collective-permute-start.25 = (bf16[80,3072]{1,0:T(8,128)(2,1)S(1)}, bf16[80,3072]{1,0:T(8,128)(2,1)S(1)}, u32[]{:S(2)}, u32[]{:S(2)}) collective-permute-start(bf16[80,3072]{1,0:T(8,128)(2,1)S(1)} %get-tuple-element.182.refs_0_), channel_id=1, source_target_pairs={{0,8},{8,16},{16,24},{24,28},{28,20},{20,12},{12,4},{4,0},{1,9},{9... | collective-permute-start | bytes 1474568 | tf_op jit(solution)/shard_map/ppermute | solution.py:284
  36.9 1.6 collective-permute-start.24
  38.6 8.6 %collective-permute-done.23.refs_4_ = bf16[80,1536]{1,0:T(8,128)(2,1)S(1)} collective-permute-done((bf16[80,1536]{1,0:T(8,128)(2,1)S(1)}, bf16[80,1536]{1,0:T(8,128)(2,1)S(1)}, u32[]{:S(2)}, u32[]{:S(2)}) %collective-permute-start.23) | collective-permute-done | bytes 245792 | tf_op jit(solution)/shard_map/ppermute | solution.py:284
  47.2 1.4 collective-permute-done.24.refs_4_
  48.6 0.8 collective-permute-start.27
  49.7 1.7 collective-permute-start.30
  51.4 6.1 %collective-permute-done.27.refs_5_ = bf16[80,1536]{1,0:T(8,128)(2,1)S(1)} collective-permute-done((bf16[80,1536]{1,0:T(8,128)(2,1)S(1)}, bf16[80,1536]{1,0:T(8,128)(2,1)S(1)}, u32[]{:S(2)}, u32[]{:S(2)}) %collective-permute-start.27) | collective-permute-done | bytes 245792 | tf_op jit(solution)/shard_map/ppermute | solution.py:284
  57.5 10.6 %collective-permute-done.28.refs_5_ = bf16[80,1536]{1,0:T(8,128)(2,1)S(1)} collective-permute-done((bf16[80,1536]{1,0:T(8,128)(2,1)S(1)}, bf16[80,1536]{1,0:T(8,128)(2,1)S(1)}, u32[]{:S(2)}, u32[]{:S(2)}) %collective-permute-start.28) | collective-permute-done | bytes 245792 | tf_op jit(solution)/shard_map/ppermute | solution.py:284
  68.0 0.5 collective-permute-start.36
  68.6 1.5 collective-permute-start.37
  70.1 0.5 collective-permute-start.34
  70.6 1.5 collective-permute-start.35
  72.1 10.2 %shard_map.60 = (bf16[2304,640]{1,0:T(8,128)(2,1)S(1)}, f32[8,128]{1,0:T(8,128)S(1)}) custom-call(s32[24]{0:T(128)S(1)} %dynamic-slice_bitcast_fusion.plan_ref, s32[8,128]{1,0:T(8,128)S(1)} %shard_map.58.masks_ref, bf16[256,2304]{1,0:T(8,128)(2,1)} %refs_0_.1, bf16[256,2304]{1,0:T(8,128)(2,1)S(1)} %collective-permute-done.31.refs_1_, ...), custom_call_target="tpu_custom_call" | custom-call | tf_op jit(solution)/shard_map/pallas_call | solution.py:139
  82.3 3.2 %collective-permute-done.34.refs_6_ = bf16[80,1536]{1,0:T(8,128)(2,1)S(1)} collective-permute-done((bf16[80,1536]{1,0:T(8,128)(2,1)S(1)}, bf16[80,1536]{1,0:T(8,128)(2,1)S(1)}, u32[]{:S(2)}, u32[]{:S(2)}) %collective-permute-start.34) | collective-permute-done | bytes 245792 | tf_op jit(solution)/shard_map/ppermute | solution.py:284
  85.8 1.1 collective-permute-start.40
  86.9 0.9 collective-permute-start.41
  87.8 1.1 collective-permute-start.38
  88.9 0.9 collective-permute-start.39
  89.8 12.3 %collective-permute-done.38.refs_7_ = bf16[80,1536]{1,0:T(8,128)(2,1)S(1)} collective-permute-done((bf16[80,1536]{1,0:T(8,128)(2,1)S(1)}, bf16[80,1536]{1,0:T(8,128)(2,1)S(1)}, u32[]{:S(2)}, u32[]{:S(2)}) %collective-permute-start.38) | collective-permute-done | bytes 245792 | tf_op jit(solution)/shard_map/ppermute | solution.py:284
  102.1 0.9 collective-permute-done.39.refs_7_
  103.5 1.5 collective-permute-start.43
  105.0 9.1 %shard_map.61 = (f32[2304,9216]{1,0:T(8,128)}, f32[8,128]{1,0:T(8,128)S(1)}) custom-call(s32[24]{0:T(128)S(1)} %dynamic-slice_bitcast_fusion.plan_ref, f32[8,128]{1,0:T(8,128)S(1)} %get-tuple-element.161.most_ref, bf16[2304,640]{1,0:T(8,128)(2,1)S(1)} %get-tuple-element.162.panel_ref, bf16[80,1536]{1,0:T(8,128)(2,1)S(1)} %get-tuple-element.171.refs_0_, ...), custom_call_target="tpu_custom_call" | custom-call | flops 4529848320 | bytes 19070976 | tf_op jit(solution)/shard_map/pallas_call | solution.py:206
  114.1 0.5 collective-permute-start.44
  114.6 1.5 collective-permute-start.45
  116.1 9.1 %shard_map.62 = (f32[2304,9216]{1,0:T(8,128)}, f32[8,128]{1,0:T(8,128)S(1)}) custom-call(s32[24]{0:T(128)S(1)} %dynamic-slice_bitcast_fusion.plan_ref, f32[8,128]{1,0:T(8,128)S(1)} %get-tuple-element.172.most_ref, bf16[2304,640]{1,0:T(8,128)(2,1)S(1)} %get-tuple-element.162.panel_ref, ...), custom_call_target="tpu_custom_call", output_to_operand_aliasing={{0}: (11, {})} | custom-call | flops 4529848320 | bytes 19070976 | tf_op jit(solution)/shard_map/pallas_call | solution.py:206
  125.2 0.5 collective-permute-start.46
  125.7 1.5 collective-permute-start.47
  127.2 6.8 %collective-permute-done.46.refs_7_ = bf16[80,3072]{1,0:T(8,128)(2,1)S(1)} collective-permute-done((bf16[80,3072]{1,0:T(8,128)(2,1)S(1)}, bf16[80,3072]{1,0:T(8,128)(2,1)S(1)}, u32[]{:S(2)}, u32[]{:S(2)}) %collective-permute-start.46) | collective-permute-done | bytes 491552 | tf_op jit(solution)/shard_map/ppermute | solution.py:284
  134.0 0.5 collective-permute-done.47.refs_7_
  134.5 15.8 %shard_map.63 = (f32[2304,9216]{1,0:T(8,128)}, f32[8,128]{1,0:T(8,128)S(1)}) custom-call(s32[24]{0:T(128)S(1)} %dynamic-slice_bitcast_fusion.plan_ref, f32[8,128]{1,0:T(8,128)S(1)} %get-tuple-element.177.most_ref, bf16[2304,640]{1,0:T(8,128)(2,1)S(1)} %get-tuple-element.162.panel_ref, ...), custom_call_target="tpu_custom_call", output_to_operand_aliasing={{0}: (11, {})} | custom-call | flops 9059696640 | bytes 35192832 | tf_op jit(solution)/shard_map/pallas_call | solution.py:206
  150.3 15.8 %shard_map.64 = (f32[2304,9216]{1,0:T(8,128)}, f32[8,128]{1,0:T(8,128)S(1)}) custom-call(s32[24]{0:T(128)S(1)} %dynamic-slice_bitcast_fusion.plan_ref, f32[8,128]{1,0:T(8,128)S(1)} %get-tuple-element.184.most_ref, bf16[2304,640]{1,0:T(8,128)(2,1)S(1)} %get-tuple-element.162.panel_ref, ...), custom_call_target="tpu_custom_call", output_to_operand_aliasing={{0}: (11, {})} | custom-call | flops 9059696640 | bytes 35192832 | tf_op jit(solution)/shard_map/pallas_call | solution.py:206
  166.1 0.6 slice.3
  (43 shorter events, 3.1 us)
Async XLA Ops:
  0.0 127.2 %copy-start.9 = (s32[128]{0:T(128)S(1)}, s32[128]{0:T(128)}, u32[]{:S(2)}) copy-start(s32[128]{0:T(128)} %param.8) | copy-start | bytes 1540
  3.8 33.1 %collective-permute-start.32 = (bf16[256,2304]{1,0:T(8,128)(2,1)}, bf16[256,2304]{1,0:T(8,128)(2,1)S(1)}, u32[]{:S(2)}, u32[]{:S(2)}) collective-permute-start(bf16[256,2304]{1,0:T(8,128)(2,1)} %refs_0_.1), channel_id=1, source_target_pairs={{0,2},{1,3},{2,0},{3,1},{4,6},{5,7},{6,4},{7,5},{8,10},{9,11},{10,... | collective-permute-start | bytes 3538952 | tf_op jit(solution)/shard_map/ppermute | solution.py:266
  6.9 8.1 %collective-permute-start.15 = (bf16[80,1536]{1,0:T(8,128)(2,1)S(1)}, bf16[80,1536]{1,0:T(8,128)(2,1)S(1)}, u32[]{:S(2)}, u32[]{:S(2)}) collective-permute-start(bf16[80,1536]{1,0:T(8,128)(2,1)S(1)} %get-tuple-element.171.refs_0_), channel_id=1, source_target_pairs={{0,8},{8,16},{16,24},{24,28},{28,20},{20,12},{12,4},{4,0},{1,9},{9... | collective-permute-start | bytes 737288 | tf_op jit(solution)/shard_map/ppermute | solution.py:284
  8.4 7.1 %collective-permute-start.16 = (bf16[80,1536]{1,0:T(8,128)(2,1)S(1)}, bf16[80,1536]{1,0:T(8,128)(2,1)S(1)}, u32[]{:S(2)}, u32[]{:S(2)}) collective-permute-start(bf16[80,1536]{1,0:T(8,128)(2,1)S(1)} %get-tuple-element.175.refs_0_), channel_id=1, source_target_pairs={{8,0},{16,8},{24,16},{28,24},{20,28},{12,20},{4,12},{0,4},{9,1},{1... | collective-permute-start | bytes 737288 | tf_op jit(solution)/shard_map/ppermute | solution.py:284
  8.9 5.5 %collective-permute-start.14 = (s32[1,128]{1,0:T(1,128)}, s32[1,128]{1,0:T(1,128)S(1)}, u32[]{:S(2)}, u32[]{:S(2)}) collective-permute-start(s32[1,128]{1,0:T(1,128)} %bitcast.16), channel_id=1, source_target_pairs={{0,4},{4,0},{8,12},{12,8},{16,20},{20,16},{24,28},{28,24},{1,5},{5... | collective-permute-start | bytes 1544 | tf_op jit(solution)/shard_map/ppermute | solution.py:266
  15.6 7.8 %collective-permute-start.18 = (bf16[80,1536]{1,0:T(8,128)(2,1)S(1)}, bf16[80,1536]{1,0:T(8,128)(2,1)S(1)}, u32[]{:S(2)}, u32[]{:S(2)}) collective-permute-start(bf16[80,1536]{1,0:T(8,128)(2,1)S(1)} %collective-permute-done.15.refs_1_), channel_id=1, source_target_pairs={{0,8},{8,16},{16,24},{24,28},{28,20},{20,12},{12,4},{4,0},{1,9},{9... | collective-permute-start | bytes 737288 | tf_op jit(solution)/shard_map/ppermute | solution.py:284
  17.1 6.3 %collective-permute-start.19 = (bf16[80,1536]{1,0:T(8,128)(2,1)S(1)}, bf16[80,1536]{1,0:T(8,128)(2,1)S(1)}, u32[]{:S(2)}, u32[]{:S(2)}) collective-permute-start(bf16[80,1536]{1,0:T(8,128)(2,1)S(1)} %collective-permute-done.16.refs_1_), channel_id=1, source_target_pairs={{8,0},{16,8},{24,16},{28,24},{20,28},{12,20},{4,12},{0,4},{9,1},{1... | collective-permute-start | bytes 737288 | tf_op jit(solution)/shard_map/ppermute | solution.py:284
  17.6 5.8 %collective-permute-start.17 = (s32[2,128]{1,0:T(2,128)S(1)}, s32[2,128]{1,0:T(2,128)S(1)}, u32[]{:S(2)}, u32[]{:S(2)}) collective-permute-start(s32[2,128]{1,0:T(2,128)S(1)} %shard_map.56.one_ref), channel_id=1, source_target_pairs={{0,8},{4,12},{8,0},{12,4},{16,24},{20,28},{24,16},{28,20},{1,9},{5... | collective-permute-start | bytes 3080 | tf_op jit(solution)/shard_map/ppermute | solution.py:266
  23.4 11.0 %collective-permute-start.21 = (bf16[80,1536]{1,0:T(8,128)(2,1)S(1)}, bf16[80,1536]{1,0:T(8,128)(2,1)S(1)}, u32[]{:S(2)}, u32[]{:S(2)}) collective-permute-start(bf16[80,1536]{1,0:T(8,128)(2,1)S(1)} %collective-permute-done.18.refs_2_), channel_id=1, source_target_pairs={{0,8},{8,16},{16,24},{24,28},{28,20},{20,12},{12,4},{4,0},{1,9},{9... | collective-permute-start | bytes 737288 | tf_op jit(solution)/shard_map/ppermute | solution.py:284
  25.2 9.2 %collective-permute-start.22 = (bf16[80,1536]{1,0:T(8,128)(2,1)S(1)}, bf16[80,1536]{1,0:T(8,128)(2,1)S(1)}, u32[]{:S(2)}, u32[]{:S(2)}) collective-permute-start(bf16[80,1536]{1,0:T(8,128)(2,1)S(1)} %collective-permute-done.19.refs_2_), channel_id=1, source_target_pairs={{8,0},{16,8},{24,16},{28,24},{20,28},{12,20},{4,12},{0,4},{9,1},{1... | collective-permute-start | bytes 737288 | tf_op jit(solution)/shard_map/ppermute | solution.py:284
  25.5 8.9 %collective-permute-start.20 = (s32[4,128]{1,0:T(4,128)S(1)}, s32[4,128]{1,0:T(4,128)S(1)}, u32[]{:S(2)}, u32[]{:S(2)}) collective-permute-start(s32[4,128]{1,0:T(4,128)S(1)} %shard_map.57.one_ref), channel_id=1, source_target_pairs={{0,16},{4,20},{8,24},{12,28},{16,0},{20,4},{24,8},{28,12},{1,17},{... | collective-permute-start | bytes 6152 | tf_op jit(solution)/shard_map/ppermute | solution.py:266
  34.4 14.2 %collective-permute-start.26 = (bf16[80,3072]{1,0:T(8,128)(2,1)S(1)}, bf16[80,3072]{1,0:T(8,128)(2,1)S(1)}, u32[]{:S(2)}, u32[]{:S(2)}) collective-permute-start(bf16[80,3072]{1,0:T(8,128)(2,1)S(1)} %get-tuple-element.185.refs_0_), channel_id=1, source_target_pairs={{8,0},{16,8},{24,16},{28,24},{20,28},{12,20},{4,12},{0,4},{9,1},{1... | collective-permute-start | bytes 1474568 | tf_op jit(solution)/shard_map/ppermute | solution.py:284
  34.5 14.1 %collective-permute-start.25 = (bf16[80,3072]{1,0:T(8,128)(2,1)S(1)}, bf16[80,3072]{1,0:T(8,128)(2,1)S(1)}, u32[]{:S(2)}, u32[]{:S(2)}) collective-permute-start(bf16[80,3072]{1,0:T(8,128)(2,1)S(1)} %get-tuple-element.182.refs_0_), channel_id=1, source_target_pairs={{0,8},{8,16},{16,24},{24,28},{28,20},{20,12},{12,4},{4,0},{1,9},{9... | collective-permute-start | bytes 1474568 | tf_op jit(solution)/shard_map/ppermute | solution.py:284
  36.5 10.7 %collective-permute-start.23 = (bf16[80,1536]{1,0:T(8,128)(2,1)S(1)}, bf16[80,1536]{1,0:T(8,128)(2,1)S(1)}, u32[]{:S(2)}, u32[]{:S(2)}) collective-permute-start(bf16[80,1536]{1,0:T(8,128)(2,1)S(1)} %collective-permute-done.21.refs_3_), channel_id=1, source_target_pairs={{0,8},{8,16},{16,24},{24,28},{28,20},{20,12},{12,4},{4,0},{1,9},{9... | collective-permute-start | bytes 737288 | tf_op jit(solution)/shard_map/ppermute | solution.py:284
  36.9 33.6 %collective-permute-start.31 = (bf16[256,2304]{1,0:T(8,128)(2,1)}, bf16[256,2304]{1,0:T(8,128)(2,1)S(1)}, u32[]{:S(2)}, u32[]{:S(2)}) collective-permute-start(bf16[256,2304]{1,0:T(8,128)(2,1)} %refs_0_.1), channel_id=1, source_target_pairs={{0,1},{1,0},{2,3},{3,2},{4,5},{5,4},{6,7},{7,6},{8,9},{9,8},{10,11... | collective-permute-start | bytes 3538952 | tf_op jit(solution)/shard_map/ppermute | solution.py:266
  36.9 50.0 %copy-start.6 = (bf16[256,2304]{1,0:T(8,128)(2,1)}, bf16[256,2304]{1,0:T(8,128)(2,1)S(1)}, u32[]{:S(2)}) copy-start(bf16[256,2304]{1,0:T(8,128)(2,1)S(1)} %collective-permute-done.32.refs_2_) | copy-start | bytes 3538948
  36.9 11.6 %collective-permute-start.24 = (bf16[80,1536]{1,0:T(8,128)(2,1)S(1)}, bf16[80,1536]{1,0:T(8,128)(2,1)S(1)}, u32[]{:S(2)}, u32[]{:S(2)}) collective-permute-start(bf16[80,1536]{1,0:T(8,128)(2,1)S(1)} %collective-permute-done.22.refs_3_), channel_id=1, source_target_pairs={{8,0},{16,8},{24,16},{28,24},{20,28},{12,20},{4,12},{0,4},{9,1},{1... | collective-permute-start | bytes 737288 | tf_op jit(solution)/shard_map/ppermute | solution.py:284
  47.2 24.9 %collective-permute-start.33 = (bf16[256,2304]{1,0:T(8,128)(2,1)S(1)}, bf16[256,2304]{1,0:T(8,128)(2,1)S(1)}, u32[]{:S(2)}, u32[]{:S(2)}) collective-permute-start(bf16[256,2304]{1,0:T(8,128)(2,1)S(1)} %collective-permute-done.32.refs_2_), channel_id=1, source_target_pairs={{0,1},{1,0},{2,3},{3,2},{4,5},{5,4},{6,7},{7,6},{8,9},{9,8},{10,11... | collective-permute-start | bytes 3538952 | tf_op jit(solution)/shard_map/ppermute | solution.py:266
  48.6 8.9 %collective-permute-start.27 = (bf16[80,1536]{1,0:T(8,128)(2,1)S(1)}, bf16[80,1536]{1,0:T(8,128)(2,1)S(1)}, u32[]{:S(2)}, u32[]{:S(2)}) collective-permute-start(bf16[80,1536]{1,0:T(8,128)(2,1)S(1)} %collective-permute-done.23.refs_4_), channel_id=1, source_target_pairs={{0,8},{8,16},{16,24},{24,28},{28,20},{20,12},{12,4},{4,0},{1,9},{9... | collective-permute-start | bytes 737288 | tf_op jit(solution)/shard_map/ppermute | solution.py:284
  49.4 18.7 %collective-permute-start.29 = (bf16[80,3072]{1,0:T(8,128)(2,1)S(1)}, bf16[80,3072]{1,0:T(8,128)(2,1)S(1)}, u32[]{:S(2)}, u32[]{:S(2)}) collective-permute-start(bf16[80,3072]{1,0:T(8,128)(2,1)S(1)} %collective-permute-done.25.refs_1_), channel_id=1, source_target_pairs={{0,8},{8,16},{16,24},{24,28},{28,20},{20,12},{12,4},{4,0},{1,9},{9... | collective-permute-start | bytes 1474568 | tf_op jit(solution)/shard_map/ppermute | solution.py:284
  49.7 18.3 %collective-permute-start.30 = (bf16[80,3072]{1,0:T(8,128)(2,1)S(1)}, bf16[80,3072]{1,0:T(8,128)(2,1)S(1)}, u32[]{:S(2)}, u32[]{:S(2)}) collective-permute-start(bf16[80,3072]{1,0:T(8,128)(2,1)S(1)} %collective-permute-done.26.refs_1_), channel_id=1, source_target_pairs={{8,0},{16,8},{24,16},{28,24},{20,28},{12,20},{4,12},{0,4},{9,1},{1... | collective-permute-start | bytes 1474568 | tf_op jit(solution)/shard_map/ppermute | solution.py:284
  57.5 10.6 %collective-permute-start.28 = (bf16[80,1536]{1,0:T(8,128)(2,1)S(1)}, bf16[80,1536]{1,0:T(8,128)(2,1)S(1)}, u32[]{:S(2)}, u32[]{:S(2)}) collective-permute-start(bf16[80,1536]{1,0:T(8,128)(2,1)S(1)} %collective-permute-done.24.refs_4_), channel_id=1, source_target_pairs={{8,0},{16,8},{24,16},{28,24},{20,28},{12,20},{4,12},{0,4},{9,1},{1... | collective-permute-start | bytes 737288 | tf_op jit(solution)/shard_map/ppermute | solution.py:284
  68.0 17.7 %collective-permute-start.36 = (bf16[80,3072]{1,0:T(8,128)(2,1)S(1)}, bf16[80,3072]{1,0:T(8,128)(2,1)S(1)}, u32[]{:S(2)}, u32[]{:S(2)}) collective-permute-start(bf16[80,3072]{1,0:T(8,128)(2,1)S(1)} %collective-permute-done.29.refs_2_), channel_id=1, source_target_pairs={{0,8},{8,16},{16,24},{24,28},{28,20},{20,12},{12,4},{4,0},{1,9},{9... | collective-permute-start | bytes 1474568 | tf_op jit(solution)/shard_map/ppermute | solution.py:284
  68.6 17.2 %collective-permute-start.37 = (bf16[80,3072]{1,0:T(8,128)(2,1)S(1)}, bf16[80,3072]{1,0:T(8,128)(2,1)S(1)}, u32[]{:S(2)}, u32[]{:S(2)}) collective-permute-start(bf16[80,3072]{1,0:T(8,128)(2,1)S(1)} %collective-permute-done.30.refs_2_), channel_id=1, source_target_pairs={{8,0},{16,8},{24,16},{28,24},{20,28},{12,20},{4,12},{0,4},{9,1},{1... | collective-permute-start | bytes 1474568 | tf_op jit(solution)/shard_map/ppermute | solution.py:284
  70.1 15.4 %collective-permute-start.34 = (bf16[80,1536]{1,0:T(8,128)(2,1)S(1)}, bf16[80,1536]{1,0:T(8,128)(2,1)S(1)}, u32[]{:S(2)}, u32[]{:S(2)}) collective-permute-start(bf16[80,1536]{1,0:T(8,128)(2,1)S(1)} %collective-permute-done.27.refs_5_), channel_id=1, source_target_pairs={{0,8},{8,16},{16,24},{24,28},{28,20},{20,12},{12,4},{4,0},{1,9},{9... | collective-permute-start | bytes 737288 | tf_op jit(solution)/shard_map/ppermute | solution.py:284
  70.6 16.3 %copy-start.7 = (bf16[256,2304]{1,0:T(8,128)(2,1)}, bf16[256,2304]{1,0:T(8,128)(2,1)S(1)}, u32[]{:S(2)}) copy-start(bf16[256,2304]{1,0:T(8,128)(2,1)S(1)} %collective-permute-done.31.refs_1_) | copy-start | bytes 3538948
  70.6 15.2 %collective-permute-start.35 = (bf16[80,1536]{1,0:T(8,128)(2,1)S(1)}, bf16[80,1536]{1,0:T(8,128)(2,1)S(1)}, u32[]{:S(2)}, u32[]{:S(2)}) collective-permute-start(bf16[80,1536]{1,0:T(8,128)(2,1)S(1)} %collective-permute-done.28.refs_5_), channel_id=1, source_target_pairs={{8,0},{16,8},{24,16},{28,24},{20,28},{12,20},{4,12},{0,4},{9,1},{1... | collective-permute-start | bytes 737288 | tf_op jit(solution)/shard_map/ppermute | solution.py:284
  72.1 78.2 %copy-start.8 = (bf16[256,2304]{1,0:T(8,128)(2,1)}, bf16[256,2304]{1,0:T(8,128)(2,1)S(1)}, u32[]{:S(2)}) copy-start(bf16[256,2304]{1,0:T(8,128)(2,1)S(1)} %collective-permute-done.33.refs_3_) | copy-start | bytes 3538948
  85.8 17.3 %collective-permute-start.40 = (bf16[80,3072]{1,0:T(8,128)(2,1)S(1)}, bf16[80,3072]{1,0:T(8,128)(2,1)S(1)}, u32[]{:S(2)}, u32[]{:S(2)}) collective-permute-start(bf16[80,3072]{1,0:T(8,128)(2,1)S(1)} %collective-permute-done.36.refs_3_), channel_id=1, source_target_pairs={{0,8},{8,16},{16,24},{24,28},{28,20},{20,12},{12,4},{4,0},{1,9},{9... | collective-permute-start | bytes 1474568 | tf_op jit(solution)/shard_map/ppermute | solution.py:284
  86.9 16.1 %collective-permute-start.41 = (bf16[80,3072]{1,0:T(8,128)(2,1)S(1)}, bf16[80,3072]{1,0:T(8,128)(2,1)S(1)}, u32[]{:S(2)}, u32[]{:S(2)}) collective-permute-start(bf16[80,3072]{1,0:T(8,128)(2,1)S(1)} %collective-permute-done.37.refs_3_), channel_id=1, source_target_pairs={{8,0},{16,8},{24,16},{28,24},{20,28},{12,20},{4,12},{0,4},{9,1},{1... | collective-permute-start | bytes 1474568 | tf_op jit(solution)/shard_map/ppermute | solution.py:284
  87.8 14.3 %collective-permute-start.38 = (bf16[80,1536]{1,0:T(8,128)(2,1)S(1)}, bf16[80,1536]{1,0:T(8,128)(2,1)S(1)}, u32[]{:S(2)}, u32[]{:S(2)}) collective-permute-start(bf16[80,1536]{1,0:T(8,128)(2,1)S(1)} %collective-permute-done.34.refs_6_), channel_id=1, source_target_pairs={{0,8},{8,16},{16,24},{24,28},{28,20},{20,12},{12,4},{4,0},{1,9},{9... | collective-permute-start | bytes 737288 | tf_op jit(solution)/shard_map/ppermute | solution.py:284
  88.9 14.1 %collective-permute-start.39 = (bf16[80,1536]{1,0:T(8,128)(2,1)S(1)}, bf16[80,1536]{1,0:T(8,128)(2,1)S(1)}, u32[]{:S(2)}, u32[]{:S(2)}) collective-permute-start(bf16[80,1536]{1,0:T(8,128)(2,1)S(1)} %collective-permute-done.35.refs_6_), channel_id=1, source_target_pairs={{8,0},{16,8},{24,16},{28,24},{20,28},{12,20},{4,12},{0,4},{9,1},{1... | collective-permute-start | bytes 737288 | tf_op jit(solution)/shard_map/ppermute | solution.py:284
  103.0 11.1 %collective-permute-start.42 = (bf16[80,3072]{1,0:T(8,128)(2,1)S(1)}, bf16[80,3072]{1,0:T(8,128)(2,1)S(1)}, u32[]{:S(2)}, u32[]{:S(2)}) collective-permute-start(bf16[80,3072]{1,0:T(8,128)(2,1)S(1)} %collective-permute-done.40.refs_4_), channel_id=1, source_target_pairs={{0,8},{8,16},{16,24},{24,28},{28,20},{20,12},{12,4},{4,0},{1,9},{9... | collective-permute-start | bytes 1474568 | tf_op jit(solution)/shard_map/ppermute | solution.py:284
  103.5 10.6 %collective-permute-start.43 = (bf16[80,3072]{1,0:T(8,128)(2,1)S(1)}, bf16[80,3072]{1,0:T(8,128)(2,1)S(1)}, u32[]{:S(2)}, u32[]{:S(2)}) collective-permute-start(bf16[80,3072]{1,0:T(8,128)(2,1)S(1)} %collective-permute-done.41.refs_4_), channel_id=1, source_target_pairs={{8,0},{16,8},{24,16},{28,24},{20,28},{12,20},{4,12},{0,4},{9,1},{1... | collective-permute-start | bytes 1474568 | tf_op jit(solution)/shard_map/ppermute | solution.py:284
  114.1 11.1 %collective-permute-start.44 = (bf16[80,3072]{1,0:T(8,128)(2,1)S(1)}, bf16[80,3072]{1,0:T(8,128)(2,1)S(1)}, u32[]{:S(2)}, u32[]{:S(2)}) collective-permute-start(bf16[80,3072]{1,0:T(8,128)(2,1)S(1)} %collective-permute-done.42.refs_5_), channel_id=1, source_target_pairs={{0,8},{8,16},{16,24},{24,28},{28,20},{20,12},{12,4},{4,0},{1,9},{9... | collective-permute-start | bytes 1474568 | tf_op jit(solution)/shard_map/ppermute | solution.py:284
  114.6 10.6 %collective-permute-start.45 = (bf16[80,3072]{1,0:T(8,128)(2,1)S(1)}, bf16[80,3072]{1,0:T(8,128)(2,1)S(1)}, u32[]{:S(2)}, u32[]{:S(2)}) collective-permute-start(bf16[80,3072]{1,0:T(8,128)(2,1)S(1)} %collective-permute-done.43.refs_5_), channel_id=1, source_target_pairs={{8,0},{16,8},{24,16},{28,24},{20,28},{12,20},{4,12},{0,4},{9,1},{1... | collective-permute-start | bytes 1474568 | tf_op jit(solution)/shard_map/ppermute | solution.py:284
  125.2 8.8 %collective-permute-start.46 = (bf16[80,3072]{1,0:T(8,128)(2,1)S(1)}, bf16[80,3072]{1,0:T(8,128)(2,1)S(1)}, u32[]{:S(2)}, u32[]{:S(2)}) collective-permute-start(bf16[80,3072]{1,0:T(8,128)(2,1)S(1)} %collective-permute-done.44.refs_6_), channel_id=1, source_target_pairs={{0,8},{8,16},{16,24},{24,28},{28,20},{20,12},{12,4},{4,0},{1,9},{9... | collective-permute-start | bytes 1474568 | tf_op jit(solution)/shard_map/ppermute | solution.py:284
  125.7 8.8 %collective-permute-start.47 = (bf16[80,3072]{1,0:T(8,128)(2,1)S(1)}, bf16[80,3072]{1,0:T(8,128)(2,1)S(1)}, u32[]{:S(2)}, u32[]{:S(2)}) collective-permute-start(bf16[80,3072]{1,0:T(8,128)(2,1)S(1)} %collective-permute-done.45.refs_6_), channel_id=1, source_target_pairs={{8,0},{16,8},{24,16},{28,24},{20,28},{12,20},{4,12},{0,4},{9,1},{1... | collective-permute-start | bytes 1474568 | tf_op jit(solution)/shard_map/ppermute | solution.py:284

commit v2 on v1

--- a/solution.py
+++ b/solution.py
@@ -13,9 +13,11 @@
 LANES = 128
 ROWS = 80
 SPLIT = (2, 4)
-TIGHT = True
+MASK_ROUND = 1
+PANEL_ROUND = 2
 STAGGER = 3
 LIMIT = 28 * 2**20
+WIDE_LIMIT = 40 * 2**20
 
 
 def token_weights(mask, timesteps, first, seq_len, total):
@@ -168,46 +170,59 @@
     )(one, two)
 
 
-def product_kernel(n, cap, rows, adds, line, plan_ref, most_ref, panel_ref, *refs):
-    pieces, (out_ref, mark_ref, depth_ref) = refs[:n], refs[-3:]
-    i = pl.program_id(1)
+def product_kernel(n, cap, rows, adds, lines, tiles, plan_ref, most_ref, panel_ref, *refs):
+    out_ref, mark_ref, depth_ref = refs[-3:]
+    j, i = pl.program_id(0), pl.program_id(1)
     mark_ref[...] = most_ref[...]
-
-    @pl.when(i == 0)
-    def _():
-        for j in range(n):
-            depth_ref[pl.ds(pl.multiple_of(plan_ref[line * n + j] * cap, 16), cap), :] = pieces[j][...]
+    for k, line in enumerate(lines):
+
+        @pl.when((i == 0) & (j >= k * tiles) & (j < (k + 1) * tiles))
+        def _(pieces=refs[k * n : (k + 1) * n], line=line):
+            for s in range(n):
+                at = pl.multiple_of(plan_ref[line * n + s] * cap, 16)
+                depth_ref[pl.ds(at, cap), :] = pieces[s][...]
 
     panel = panel_ref[pl.ds(pl.multiple_of(i * rows, 16), rows), :]
     result = jnp.dot(panel, depth_ref[...], preferred_element_type=jnp.float32)
     if adds:
-        result = result + refs[n][...]
+        result = result + refs[len(lines) * n][...]
     out_ref[...] = result
 
 
-def product(panel_t, most, pieces, plan, line, out, adds, first, shape):
-    n, (cap, width) = len(pieces), pieces[0].shape
+def product(panel_t, most, sides, plan, out, adds, shape):
+    pieces, lines, firsts = zip(*sides)
+    n, (cap, width) = len(pieces[0]), pieces[0][0].shape
     features, depth = panel_t.shape
     blocks = 3 if features % (3 * 16) == 0 else 1
     rows = features // blocks
-    tile = tile_of(first, width, 768 if adds else 1536)
-    place = lambda j, i, plan: (i, first // tile + j)
+    tile = min(tile_of(first, width, 768 if adds else 1536) for first in firsts)
+    tiles = width // tile
+    bases = [first // tile for first in firsts]
+
+    def place(j, i, plan):
+        column = bases[0] + j
+        for k in range(1, len(bases)):
+            column = jnp.where(j >= k * tiles, bases[k] + j - k * tiles, column)
+        return i, column
+
     specs = [
         pl.BlockSpec((8, LANES), lambda j, i, plan: (0, 0)),
         pl.BlockSpec((features, depth), lambda j, i, plan: (0, 0)),
     ]
-    specs += [pl.BlockSpec((cap, tile), lambda j, i, plan: (0, j)) for _ in pieces]
-    args = [plan, most, panel_t, *pieces]
+    for k in range(len(sides)):
+        turn = lambda j, i, plan, k=k: (0, jnp.clip(j - k * tiles, 0, tiles - 1))
+        specs += [pl.BlockSpec((cap, tile), turn)] * n
+    args = [plan, most, panel_t, *sum(pieces, [])]
     aliases = {}
     if out is not None:
         specs.append(pl.BlockSpec((rows, tile), place) if adds else pl.BlockSpec(memory_space=pl.ANY))
         args.append(out)
         aliases = {len(args) - 1: 0}
     return pl.pallas_call(
-        functools.partial(product_kernel, n, cap, rows, adds, line),
+        functools.partial(product_kernel, n, cap, rows, adds, lines, tiles),
         grid_spec=pltpu.PrefetchScalarGridSpec(
             num_scalar_prefetch=1,
-            grid=(width // tile, blocks),
+            grid=(len(sides) * tiles, blocks),
             in_specs=specs,
             out_specs=[
                 pl.BlockSpec((rows, tile), place),
@@ -220,10 +235,10 @@
             jax.ShapeDtypeStruct((8, LANES), jnp.float32),
         ],
         input_output_aliases=aliases,
-        compiler_params=pltpu.CompilerParams(vmem_limit_bytes=LIMIT),
+        compiler_params=pltpu.CompilerParams(vmem_limit_bytes=LIMIT if len(sides) == 1 else WIDE_LIMIT),
         cost_estimate=pl.CostEstimate(
-            flops=2 * features * depth * width,
-            bytes_accessed=features * (4 * width + 2 * depth) + 2 * depth * width,
+            flops=2 * features * depth * width * len(sides),
+            bytes_accessed=(features * 4 + 2 * depth) * width * len(sides) + 2 * features * depth,
             transcendentals=0,
         ),
     )(*args)
@@ -280,30 +295,33 @@
             step = r - STAGGER * k
             if 1 <= step < n:
                 for ring, perm in zip(rings[k], (fore, back)):
-                    tied = marks + (before if TIGHT or step == 1 else [])
+                    tied = marks + before
                     ring.append(lax.ppermute(after(ring[-1], *tied), "row", perm))
                     fresh.append(ring[-1])
-        if bit < n:
+        if bit < n and r >= MASK_ROUND:
             masks = join(masks, swap(after(masks, *before), "row", n, bit))
             fresh.append(masks)
             bit *= 2
-        if r == 1 and cols == 4:
+        if r == PANEL_ROUND and cols == 4:
             parts.append(swap(after(panel, *before), "col", cols, 1))
             parts.append(swap(after(panel, *before), "col", cols, 2))
-        elif r == 1:
+        elif r == PANEL_ROUND:
             parts = [lax.all_gather(panel, "col", axis=0, tiled=True)]
-        if r == max(n - 4, 2) and cols == 4:
+        if r == max(n - 3, 2) and cols == 4:
             parts.append(swap(after(parts[2], *before), "col", cols, 1))
         marks = []
-        if r == n - 2:
+        if r == n - 1:
             panel_t, most = select(parts, after(masks, *before), plan, 0, cap)
             marks = [most]
         for k in range(chunks):
-            side = r - STAGGER * k - n
-            if 0 <= side < 2:
-                pieces = rings[k][side]
-                pieces = [after(pieces[0], *before), *pieces[1:]]
-                out, most = product(panel_t, most, pieces, plan, side, out, False, spans[side][k][0], shape)
+            due = r - STAGGER * k - n
+            sides = [(rings[k][side], side, spans[side][k][0]) for side in range(2)]
+            if k < chunks - 1 or spans[0][k][1] != spans[1][k][1]:
+                sides = sides[due : due + 1]
+            if sides and 0 <= due < 3 - len(sides):
+                pieces = sides[0][0]
+                sides[0] = ([after(pieces[0], *before), *pieces[1:]], *sides[0][1:])
+                out, most = product(panel_t, most, sides, plan, out, False, shape)
                 marks.append(most)
         before = fresh or before
     if cap == per:
@@ -318,7 +336,7 @@
             pieces = [piece]
             for _ in range(n - 1):
                 pieces.append(lax.ppermute(pieces[-1], "row", perm))
-            out, mark = product(panel_t, mark, pieces, plan, line, out, True, span[0][0], shape)
+            out, mark = product(panel_t, mark, [(pieces, line, span[0][0])], plan, out, True, shape)
         return out
 
     return lax.fori_loop(0, (most[0, 0] > cap).astype(jnp.int32), rest, out)

time: 168 us -> 163 us (0.970)
  waiting for transfers between devices: 61.8 us -> 59.3 us
  Pallas kernels: 65.4 us -> 63 us
    pallas_call x4 -> x3, Pallas kernels: 49.6 us -> 47.2 us  [product(): pl.pallas_call(functools.partial(product_kernel, n, cap, rows, adds, line...]
    ppermute x6, waiting for transfers between devices: 10.6 us -> 8.84 us  [swap(): return lax.ppermute(value, axis, [(i, i ^ bit) for i in range(size)])]
  transfers between devices with their start and end apart: 34 -> 34, of which waited for: 14 -> 14; matrix products, arithmetic and copies ran while one was open for 0% -> 0% of each run, Pallas kernels for 19% -> 20%
where the time goes in v2:
time: 163 us
  Pallas kernels  63 us (39%)
  waiting for transfers between devices  59.3 us (36%)
  starting transfers between devices  36.7 us (23%)
    ppermute x28, waiting for transfers between devices, body(): ring.append(lax.ppermute(after(ring[-1], *tied), 'row', perm))  50.5 us
    pallas_call x3, Pallas kernels, product(): pl.pallas_call(functools.partial(product_kernel, n, cap, rows, adds, line...  47.2 us
    ppermute x28, starting transfers between devices, body(): ring.append(lax.ppermute(after(ring[-1], *tied), 'row', perm))  28.5 us
    pallas_call x1, Pallas kernels, select(): pl.pallas_call(functools.partial(select_kernel, base, rows), grid_spec=pl...  10.2 us
    ppermute x6, waiting for transfers between devices, swap(): return lax.ppermute(value, axis, [(i, i ^ bit) for i in range(size)])  8.84 us
    ppermute x6, starting transfers between devices, swap(): return lax.ppermute(value, axis, [(i, i ^ bit) for i in range(size)])  8.28 us
    pallas_call x2, Pallas kernels, pack(): pl.pallas_call(functools.partial(pack_kernel, base, rows, unit, ranges),...  4.96 us
  transfers between devices with their start and end apart: 34, of which 14 were waited for; matrix products, arithmetic and copies ran while one was open for 0% of the time, Pallas kernels for 20%

profile of v2, /device:TPU:0, one launch (start us, length us, event | category | flops | bytes accessed | tf_op | source)
XLA Modules:
  0.0 162.8 jit_solution(12279263341241953950)
XLA Ops:
  0.7 0.7 dynamic-slice_bitcast_fusion.plan_ref
  1.4 0.7 fusion.3.weight_ref
  2.0 1.8 %shard_map.55 = (bf16[80,1536]{1,0:T(8,128)(2,1)S(1)}, bf16[80,1536]{1,0:T(8,128)(2,1)S(1)}) custom-call(s32[1,128]{1,0:T(1,128)} %bitcast.15, f32[1,128]{1,0:T(1,128)S(1)} %fusion.3.weight_ref, bf16[128,9216]{1,0:T(8,128)(2,1)} %cot_ref.1), custom_call_target="tpu_custom_call" | custom-call | tf_op jit(solution)/shard_map/pallas_call | solution.py:103
  3.8 3.1 %collective-permute-start.15 = (bf16[80,1536]{1,0:T(8,128)(2,1)S(1)}, bf16[80,1536]{1,0:T(8,128)(2,1)S(1)}, u32[]{:S(2)}, u32[]{:S(2)}) collective-permute-start(bf16[80,1536]{1,0:T(8,128)(2,1)S(1)} %get-tuple-element.168.refs_0_), channel_id=1, source_target_pairs={{0,8},{8,16},{16,24},{24,28},{28,20},{20,12},{12,4},{4,0},{1,9},{9... | collective-permute-start | bytes 737288 | tf_op jit(solution)/shard_map/ppermute | solution.py:299
  6.9 1.9 %collective-permute-start.14 = (s32[1,128]{1,0:T(1,128)}, s32[1,128]{1,0:T(1,128)S(1)}, u32[]{:S(2)}, u32[]{:S(2)}) collective-permute-start(s32[1,128]{1,0:T(1,128)} %bitcast.16), channel_id=1, source_target_pairs={{0,4},{4,0},{8,12},{12,8},{16,20},{20,16},{24,28},{28,24},{1,5},{5... | collective-permute-start | bytes 1544 | tf_op jit(solution)/shard_map/ppermute | solution.py:281
  8.8 4.0 %collective-permute-done.14.two_ref = s32[1,128]{1,0:T(1,128)S(1)} collective-permute-done((s32[1,128]{1,0:T(1,128)}, s32[1,128]{1,0:T(1,128)S(1)}, u32[]{:S(2)}, u32[]{:S(2)}) %collective-permute-start.14) | collective-permute-done | bytes 544 | tf_op jit(solution)/shard_map/ppermute | solution.py:281
  12.8 0.7 shard_map.56.one_ref
  13.5 0.8 collective-permute-done.16.refs_1_
  14.3 1.6 collective-permute-start.18
  16.3 1.5 collective-permute-start.36
  17.9 1.6 collective-permute-start.17
  19.4 2.7 %collective-permute-done.17.two_ref = s32[2,128]{1,0:T(2,128)S(1)} collective-permute-done((s32[2,128]{1,0:T(2,128)S(1)}, s32[2,128]{1,0:T(2,128)S(1)}, u32[]{:S(2)}, u32[]{:S(2)}) %collective-permute-start.17) | collective-permute-done | bytes 1056 | tf_op jit(solution)/shard_map/ppermute | solution.py:281
  22.2 2.0 %collective-permute-start.21 = (bf16[80,1536]{1,0:T(8,128)(2,1)S(1)}, bf16[80,1536]{1,0:T(8,128)(2,1)S(1)}, u32[]{:S(2)}, u32[]{:S(2)}) collective-permute-start(bf16[80,1536]{1,0:T(8,128)(2,1)S(1)} %collective-permute-done.18.refs_2_), channel_id=1, source_target_pairs={{0,8},{8,16},{16,24},{24,28},{28,20},{20,12},{12,4},{4,0},{1,9},{9... | collective-permute-start | bytes 737288 | tf_op jit(solution)/shard_map/ppermute | solution.py:299
  24.3 3.2 %collective-permute-start.20 = (s32[4,128]{1,0:T(4,128)S(1)}, s32[4,128]{1,0:T(4,128)S(1)}, u32[]{:S(2)}, u32[]{:S(2)}) collective-permute-start(s32[4,128]{1,0:T(4,128)S(1)} %shard_map.57.one_ref), channel_id=1, source_target_pairs={{0,16},{4,20},{8,24},{12,28},{16,0},{20,4},{24,8},{28,12},{1,17},{... | collective-permute-start | bytes 6152 | tf_op jit(solution)/shard_map/ppermute | solution.py:281
  27.5 3.2 %shard_map.59 = (bf16[80,3072]{1,0:T(8,128)(2,1)S(1)}, bf16[80,3072]{1,0:T(8,128)(2,1)S(1)}) custom-call(s32[1,128]{1,0:T(1,128)} %bitcast.18, f32[1,128]{1,0:T(1,128)S(1)} %fusion.3.weight_ref, bf16[128,9216]{1,0:T(8,128)(2,1)} %cot_ref.1), custom_call_target="tpu_custom_call" | custom-call | tf_op jit(solution)/shard_map/pallas_call | solution.py:103
  30.7 2.1 %collective-permute-done.20.two_ref = s32[4,128]{1,0:T(4,128)S(1)} collective-permute-done((s32[4,128]{1,0:T(4,128)S(1)}, s32[4,128]{1,0:T(4,128)S(1)}, u32[]{:S(2)}, u32[]{:S(2)}) %collective-permute-start.20) | collective-permute-done | bytes 2080 | tf_op jit(solution)/shard_map/ppermute | solution.py:281
  32.9 2.0 %collective-permute-start.25 = (bf16[80,3072]{1,0:T(8,128)(2,1)S(1)}, bf16[80,3072]{1,0:T(8,128)(2,1)S(1)}, u32[]{:S(2)}, u32[]{:S(2)}) collective-permute-start(bf16[80,3072]{1,0:T(8,128)(2,1)S(1)} %get-tuple-element.179.refs_0_), channel_id=1, source_target_pairs={{0,8},{8,16},{16,24},{24,28},{28,20},{20,12},{12,4},{4,0},{1,9},{9... | collective-permute-start | bytes 1474568 | tf_op jit(solution)/shard_map/ppermute | solution.py:299
  34.9 1.0 collective-permute-start.23
  35.9 1.0 collective-permute-start.24
  36.9 12.1 %collective-permute-done.23.refs_4_ = bf16[80,1536]{1,0:T(8,128)(2,1)S(1)} collective-permute-done((bf16[80,1536]{1,0:T(8,128)(2,1)S(1)}, bf16[80,1536]{1,0:T(8,128)(2,1)S(1)}, u32[]{:S(2)}, u32[]{:S(2)}) %collective-permute-start.23) | collective-permute-done | bytes 245792 | tf_op jit(solution)/shard_map/ppermute | solution.py:299
  49.1 1.3 collective-permute-start.29
  50.4 0.7 collective-permute-start.30
  51.2 1.3 collective-permute-start.27
  52.4 0.8 collective-permute-start.28
  53.2 8.9 %collective-permute-done.27.refs_5_ = bf16[80,1536]{1,0:T(8,128)(2,1)S(1)} collective-permute-done((bf16[80,1536]{1,0:T(8,128)(2,1)S(1)}, bf16[80,1536]{1,0:T(8,128)(2,1)S(1)}, u32[]{:S(2)}, u32[]{:S(2)}) %collective-permute-start.27) | collective-permute-done | bytes 245792 | tf_op jit(solution)/shard_map/ppermute | solution.py:299
  62.1 2.4 %collective-permute-done.28.refs_5_ = bf16[80,1536]{1,0:T(8,128)(2,1)S(1)} collective-permute-done((bf16[80,1536]{1,0:T(8,128)(2,1)S(1)}, bf16[80,1536]{1,0:T(8,128)(2,1)S(1)}, u32[]{:S(2)}, u32[]{:S(2)}) %collective-permute-start.28) | collective-permute-done | bytes 245792 | tf_op jit(solution)/shard_map/ppermute | solution.py:299
  64.6 0.7 collective-permute-start.33
  65.3 1.3 collective-permute-start.34
  66.6 6.8 %collective-permute-done.31.refs_6_ = bf16[80,1536]{1,0:T(8,128)(2,1)S(1)} collective-permute-done((bf16[80,1536]{1,0:T(8,128)(2,1)S(1)}, bf16[80,1536]{1,0:T(8,128)(2,1)S(1)}, u32[]{:S(2)}, u32[]{:S(2)}) %collective-permute-start.31) | collective-permute-done | bytes 245792 | tf_op jit(solution)/shard_map/ppermute | solution.py:299
  73.4 0.7 collective-permute-start.32
  74.2 8.7 %collective-permute-done.32.refs_6_ = bf16[80,1536]{1,0:T(8,128)(2,1)S(1)} collective-permute-done((bf16[80,1536]{1,0:T(8,128)(2,1)S(1)}, bf16[80,1536]{1,0:T(8,128)(2,1)S(1)}, u32[]{:S(2)}, u32[]{:S(2)}) %collective-permute-start.32) | collective-permute-done | bytes 245792 | tf_op jit(solution)/shard_map/ppermute | solution.py:299
  82.9 0.8 collective-permute-start.40
  83.6 1.3 collective-permute-start.41
  84.9 0.8 collective-permute-start.38
  85.7 1.3 collective-permute-start.39
  86.9 10.2 %shard_map.60 = (bf16[2304,640]{1,0:T(8,128)(2,1)S(1)}, f32[8,128]{1,0:T(8,128)S(1)}) custom-call(s32[24]{0:T(128)S(1)} %dynamic-slice_bitcast_fusion.plan_ref, s32[8,128]{1,0:T(8,128)S(1)} %shard_map.58.masks_ref, bf16[256,2304]{1,0:T(8,128)(2,1)} %refs_0_.1, bf16[256,2304]{1,0:T(8,128)(2,1)S(1)} %collective-permute-done.35.refs_1_, ...), custom_call_target="tpu_custom_call" | custom-call | tf_op jit(solution)/shard_map/pallas_call | solution.py:141
  97.1 2.4 %collective-permute-done.38.refs_7_ = bf16[80,1536]{1,0:T(8,128)(2,1)S(1)} collective-permute-done((bf16[80,1536]{1,0:T(8,128)(2,1)S(1)}, bf16[80,1536]{1,0:T(8,128)(2,1)S(1)}, u32[]{:S(2)}, u32[]{:S(2)}) %collective-permute-start.38) | collective-permute-done | bytes 245792 | tf_op jit(solution)/shard_map/ppermute | solution.py:299
  99.7 1.2 collective-permute-start.42
  101.0 0.8 collective-permute-start.43
  101.8 9.1 %shard_map.61 = (f32[2304,9216]{1,0:T(8,128)}, f32[8,128]{1,0:T(8,128)S(1)}) custom-call(s32[24]{0:T(128)S(1)} %dynamic-slice_bitcast_fusion.plan_ref, f32[8,128]{1,0:T(8,128)S(1)} %get-tuple-element.162.most_ref, bf16[2304,640]{1,0:T(8,128)(2,1)S(1)} %get-tuple-element.163.panel_ref, bf16[80,1536]{1,0:T(8,128)(2,1)S(1)} %get-tuple-element.168.refs_0_, ...), custom_call_target="tpu_custom_call" | custom-call | flops 4529848320 | bytes 19070976 | tf_op jit(solution)/shard_map/pallas_call | solution.py:221
  111.0 1.0 collective-permute-start.44
  112.1 1.0 collective-permute-start.45
  113.0 9.1 %shard_map.62 = (f32[2304,9216]{1,0:T(8,128)}, f32[8,128]{1,0:T(8,128)S(1)}) custom-call(s32[24]{0:T(128)S(1)} %dynamic-slice_bitcast_fusion.plan_ref, f32[8,128]{1,0:T(8,128)S(1)} %get-tuple-element.169.most_ref, bf16[2304,640]{1,0:T(8,128)(2,1)S(1)} %get-tuple-element.163.panel_ref, ...), custom_call_target="tpu_custom_call", output_to_operand_aliasing={{0}: (11, {})} | custom-call | flops 4529848320 | bytes 19070976 | tf_op jit(solution)/shard_map/pallas_call | solution.py:221
  122.1 1.0 collective-permute-start.46
  123.2 1.0 collective-permute-start.47
  124.2 6.9 %collective-permute-done.46.refs_7_ = bf16[80,3072]{1,0:T(8,128)(2,1)S(1)} collective-permute-done((bf16[80,3072]{1,0:T(8,128)(2,1)S(1)}, bf16[80,3072]{1,0:T(8,128)(2,1)S(1)}, u32[]{:S(2)}, u32[]{:S(2)}) %collective-permute-start.46) | collective-permute-done | bytes 491552 | tf_op jit(solution)/shard_map/ppermute | solution.py:299
  131.1 1.0 collective-permute-done.47.refs_15_
  132.1 29.1 %shard_map.63 = (f32[2304,9216]{1,0:T(8,128)}, f32[8,128]{1,0:T(8,128)S(1)}) custom-call(s32[24]{0:T(128)S(1)} %dynamic-slice_bitcast_fusion.plan_ref, f32[8,128]{1,0:T(8,128)S(1)} %get-tuple-element.174.most_ref, bf16[2304,640]{1,0:T(8,128)(2,1)S(1)} %get-tuple-element.163.panel_ref, ...), custom_call_target="tpu_custom_call", output_to_operand_aliasing={{0}: (19, {})} | custom-call | flops 18119393280 | bytes 67436544 | tf_op jit(solution)/shard_map/pallas_call | solution.py:221
  (42 shorter events, 2.0 us)
Async XLA Ops:
  0.0 124.1 %copy-start.9 = (s32[128]{0:T(128)S(1)}, s32[128]{0:T(128)}, u32[]{:S(2)}) copy-start(s32[128]{0:T(128)} %param.8) | copy-start | bytes 1540
  3.8 9.7 %collective-permute-start.15 = (bf16[80,1536]{1,0:T(8,128)(2,1)S(1)}, bf16[80,1536]{1,0:T(8,128)(2,1)S(1)}, u32[]{:S(2)}, u32[]{:S(2)}) collective-permute-start(bf16[80,1536]{1,0:T(8,128)(2,1)S(1)} %get-tuple-element.168.refs_0_), channel_id=1, source_target_pairs={{0,8},{8,16},{16,24},{24,28},{28,20},{20,12},{12,4},{4,0},{1,9},{9... | collective-permute-start | bytes 737288 | tf_op jit(solution)/shard_map/ppermute | solution.py:299
  6.9 7.4 %collective-permute-start.16 = (bf16[80,1536]{1,0:T(8,128)(2,1)S(1)}, bf16[80,1536]{1,0:T(8,128)(2,1)S(1)}, u32[]{:S(2)}, u32[]{:S(2)}) collective-permute-start(bf16[80,1536]{1,0:T(8,128)(2,1)S(1)} %get-tuple-element.172.refs_0_), channel_id=1, source_target_pairs={{8,0},{16,8},{24,16},{28,24},{20,28},{12,20},{4,12},{0,4},{9,1},{1... | collective-permute-start | bytes 737288 | tf_op jit(solution)/shard_map/ppermute | solution.py:299
  6.9 5.9 %collective-permute-start.14 = (s32[1,128]{1,0:T(1,128)}, s32[1,128]{1,0:T(1,128)S(1)}, u32[]{:S(2)}, u32[]{:S(2)}) collective-permute-start(s32[1,128]{1,0:T(1,128)} %bitcast.16), channel_id=1, source_target_pairs={{0,4},{4,0},{8,12},{12,8},{16,20},{20,16},{24,28},{28,24},{1,5},{5... | collective-permute-start | bytes 1544 | tf_op jit(solution)/shard_map/ppermute | solution.py:281
  14.3 7.9 %collective-permute-start.18 = (bf16[80,1536]{1,0:T(8,128)(2,1)S(1)}, bf16[80,1536]{1,0:T(8,128)(2,1)S(1)}, u32[]{:S(2)}, u32[]{:S(2)}) collective-permute-start(bf16[80,1536]{1,0:T(8,128)(2,1)S(1)} %collective-permute-done.15.refs_1_), channel_id=1, source_target_pairs={{0,8},{8,16},{16,24},{24,28},{28,20},{20,12},{12,4},{4,0},{1,9},{9... | collective-permute-start | bytes 737288 | tf_op jit(solution)/shard_map/ppermute | solution.py:299
  15.9 6.3 %collective-permute-start.19 = (bf16[80,1536]{1,0:T(8,128)(2,1)S(1)}, bf16[80,1536]{1,0:T(8,128)(2,1)S(1)}, u32[]{:S(2)}, u32[]{:S(2)}) collective-permute-start(bf16[80,1536]{1,0:T(8,128)(2,1)S(1)} %collective-permute-done.16.refs_1_), channel_id=1, source_target_pairs={{8,0},{16,8},{24,16},{28,24},{20,28},{12,20},{4,12},{0,4},{9,1},{1... | collective-permute-start | bytes 737288 | tf_op jit(solution)/shard_map/ppermute | solution.py:299
  16.3 36.1 %collective-permute-start.36 = (bf16[256,2304]{1,0:T(8,128)(2,1)}, bf16[256,2304]{1,0:T(8,128)(2,1)S(1)}, u32[]{:S(2)}, u32[]{:S(2)}) collective-permute-start(bf16[256,2304]{1,0:T(8,128)(2,1)} %refs_0_.1), channel_id=1, source_target_pairs={{0,2},{1,3},{2,0},{3,1},{4,6},{5,7},{6,4},{7,5},{8,10},{9,11},{10,... | collective-permute-start | bytes 3538952 | tf_op jit(solution)/shard_map/ppermute | solution.py:281
  17.9 4.3 %collective-permute-start.17 = (s32[2,128]{1,0:T(2,128)S(1)}, s32[2,128]{1,0:T(2,128)S(1)}, u32[]{:S(2)}, u32[]{:S(2)}) collective-permute-start(s32[2,128]{1,0:T(2,128)S(1)} %shard_map.56.one_ref), channel_id=1, source_target_pairs={{0,8},{4,12},{8,0},{12,4},{16,24},{20,28},{24,16},{28,20},{1,9},{5... | collective-permute-start | bytes 3080 | tf_op jit(solution)/shard_map/ppermute | solution.py:281
  22.2 10.6 %collective-permute-start.21 = (bf16[80,1536]{1,0:T(8,128)(2,1)S(1)}, bf16[80,1536]{1,0:T(8,128)(2,1)S(1)}, u32[]{:S(2)}, u32[]{:S(2)}) collective-permute-start(bf16[80,1536]{1,0:T(8,128)(2,1)S(1)} %collective-permute-done.18.refs_2_), channel_id=1, source_target_pairs={{0,8},{8,16},{16,24},{24,28},{28,20},{20,12},{12,4},{4,0},{1,9},{9... | collective-permute-start | bytes 737288 | tf_op jit(solution)/shard_map/ppermute | solution.py:299
  24.1 8.7 %collective-permute-start.22 = (bf16[80,1536]{1,0:T(8,128)(2,1)S(1)}, bf16[80,1536]{1,0:T(8,128)(2,1)S(1)}, u32[]{:S(2)}, u32[]{:S(2)}) collective-permute-start(bf16[80,1536]{1,0:T(8,128)(2,1)S(1)} %collective-permute-done.19.refs_2_), channel_id=1, source_target_pairs={{8,0},{16,8},{24,16},{28,24},{20,28},{12,20},{4,12},{0,4},{9,1},{1... | collective-permute-start | bytes 737288 | tf_op jit(solution)/shard_map/ppermute | solution.py:299
  24.3 8.5 %collective-permute-start.20 = (s32[4,128]{1,0:T(4,128)S(1)}, s32[4,128]{1,0:T(4,128)S(1)}, u32[]{:S(2)}, u32[]{:S(2)}) collective-permute-start(s32[4,128]{1,0:T(4,128)S(1)} %shard_map.57.one_ref), channel_id=1, source_target_pairs={{0,16},{4,20},{8,24},{12,28},{16,0},{20,4},{24,8},{28,12},{1,17},{... | collective-permute-start | bytes 6152 | tf_op jit(solution)/shard_map/ppermute | solution.py:281
  32.8 16.2 %collective-permute-start.26 = (bf16[80,3072]{1,0:T(8,128)(2,1)S(1)}, bf16[80,3072]{1,0:T(8,128)(2,1)S(1)}, u32[]{:S(2)}, u32[]{:S(2)}) collective-permute-start(bf16[80,3072]{1,0:T(8,128)(2,1)S(1)} %get-tuple-element.150.refs_8_), channel_id=1, source_target_pairs={{8,0},{16,8},{24,16},{28,24},{20,28},{12,20},{4,12},{0,4},{9,1},{1... | collective-permute-start | bytes 1474568 | tf_op jit(solution)/shard_map/ppermute | solution.py:299
  32.9 16.2 %collective-permute-start.25 = (bf16[80,3072]{1,0:T(8,128)(2,1)S(1)}, bf16[80,3072]{1,0:T(8,128)(2,1)S(1)}, u32[]{:S(2)}, u32[]{:S(2)}) collective-permute-start(bf16[80,3072]{1,0:T(8,128)(2,1)S(1)} %get-tuple-element.179.refs_0_), channel_id=1, source_target_pairs={{0,8},{8,16},{16,24},{24,28},{28,20},{20,12},{12,4},{4,0},{1,9},{9... | collective-permute-start | bytes 1474568 | tf_op jit(solution)/shard_map/ppermute | solution.py:299
  34.9 14.2 %collective-permute-start.23 = (bf16[80,1536]{1,0:T(8,128)(2,1)S(1)}, bf16[80,1536]{1,0:T(8,128)(2,1)S(1)}, u32[]{:S(2)}, u32[]{:S(2)}) collective-permute-start(bf16[80,1536]{1,0:T(8,128)(2,1)S(1)} %collective-permute-done.21.refs_3_), channel_id=1, source_target_pairs={{0,8},{8,16},{16,24},{24,28},{28,20},{20,12},{12,4},{4,0},{1,9},{9... | collective-permute-start | bytes 737288 | tf_op jit(solution)/shard_map/ppermute | solution.py:299
  35.9 13.1 %collective-permute-start.24 = (bf16[80,1536]{1,0:T(8,128)(2,1)S(1)}, bf16[80,1536]{1,0:T(8,128)(2,1)S(1)}, u32[]{:S(2)}, u32[]{:S(2)}) collective-permute-start(bf16[80,1536]{1,0:T(8,128)(2,1)S(1)} %collective-permute-done.22.refs_3_), channel_id=1, source_target_pairs={{8,0},{16,8},{24,16},{28,24},{20,28},{12,20},{4,12},{0,4},{9,1},{1... | collective-permute-start | bytes 737288 | tf_op jit(solution)/shard_map/ppermute | solution.py:299
  49.1 15.4 %collective-permute-start.29 = (bf16[80,3072]{1,0:T(8,128)(2,1)S(1)}, bf16[80,3072]{1,0:T(8,128)(2,1)S(1)}, u32[]{:S(2)}, u32[]{:S(2)}) collective-permute-start(bf16[80,3072]{1,0:T(8,128)(2,1)S(1)} %collective-permute-done.25.refs_1_), channel_id=1, source_target_pairs={{0,8},{8,16},{16,24},{24,28},{28,20},{20,12},{12,4},{4,0},{1,9},{9... | collective-permute-start | bytes 1474568 | tf_op jit(solution)/shard_map/ppermute | solution.py:299
  50.4 14.1 %collective-permute-start.30 = (bf16[80,3072]{1,0:T(8,128)(2,1)S(1)}, bf16[80,3072]{1,0:T(8,128)(2,1)S(1)}, u32[]{:S(2)}, u32[]{:S(2)}) collective-permute-start(bf16[80,3072]{1,0:T(8,128)(2,1)S(1)} %collective-permute-done.26.refs_9_), channel_id=1, source_target_pairs={{8,0},{16,8},{24,16},{28,24},{20,28},{12,20},{4,12},{0,4},{9,1},{1... | collective-permute-start | bytes 1474568 | tf_op jit(solution)/shard_map/ppermute | solution.py:299
  51.2 10.9 %collective-permute-start.27 = (bf16[80,1536]{1,0:T(8,128)(2,1)S(1)}, bf16[80,1536]{1,0:T(8,128)(2,1)S(1)}, u32[]{:S(2)}, u32[]{:S(2)}) collective-permute-start(bf16[80,1536]{1,0:T(8,128)(2,1)S(1)} %collective-permute-done.23.refs_4_), channel_id=1, source_target_pairs={{0,8},{8,16},{16,24},{24,28},{28,20},{20,12},{12,4},{4,0},{1,9},{9... | collective-permute-start | bytes 737288 | tf_op jit(solution)/shard_map/ppermute | solution.py:299
  52.4 33.2 %collective-permute-start.35 = (bf16[256,2304]{1,0:T(8,128)(2,1)}, bf16[256,2304]{1,0:T(8,128)(2,1)S(1)}, u32[]{:S(2)}, u32[]{:S(2)}) collective-permute-start(bf16[256,2304]{1,0:T(8,128)(2,1)} %refs_0_.1), channel_id=1, source_target_pairs={{0,1},{1,0},{2,3},{3,2},{4,5},{5,4},{6,7},{7,6},{8,9},{9,8},{10,11... | collective-permute-start | bytes 3538952 | tf_op jit(solution)/shard_map/ppermute | solution.py:281
  52.4 49.3 %copy-start.6 = (bf16[256,2304]{1,0:T(8,128)(2,1)}, bf16[256,2304]{1,0:T(8,128)(2,1)S(1)}, u32[]{:S(2)}) copy-start(bf16[256,2304]{1,0:T(8,128)(2,1)S(1)} %collective-permute-done.36.refs_2_) | copy-start | bytes 3538948
  52.4 12.1 %collective-permute-start.28 = (bf16[80,1536]{1,0:T(8,128)(2,1)S(1)}, bf16[80,1536]{1,0:T(8,128)(2,1)S(1)}, u32[]{:S(2)}, u32[]{:S(2)}) collective-permute-start(bf16[80,1536]{1,0:T(8,128)(2,1)S(1)} %collective-permute-done.24.refs_4_), channel_id=1, source_target_pairs={{8,0},{16,8},{24,16},{28,24},{20,28},{12,20},{4,12},{0,4},{9,1},{1... | collective-permute-start | bytes 737288 | tf_op jit(solution)/shard_map/ppermute | solution.py:299
  62.1 24.8 %collective-permute-start.37 = (bf16[256,2304]{1,0:T(8,128)(2,1)S(1)}, bf16[256,2304]{1,0:T(8,128)(2,1)S(1)}, u32[]{:S(2)}, u32[]{:S(2)}) collective-permute-start(bf16[256,2304]{1,0:T(8,128)(2,1)S(1)} %collective-permute-done.36.refs_2_), channel_id=1, source_target_pairs={{0,1},{1,0},{2,3},{3,2},{4,5},{5,4},{6,7},{7,6},{8,9},{9,8},{10,11... | collective-permute-start | bytes 3538952 | tf_op jit(solution)/shard_map/ppermute | solution.py:281
  64.5 8.9 %collective-permute-start.31 = (bf16[80,1536]{1,0:T(8,128)(2,1)S(1)}, bf16[80,1536]{1,0:T(8,128)(2,1)S(1)}, u32[]{:S(2)}, u32[]{:S(2)}) collective-permute-start(bf16[80,1536]{1,0:T(8,128)(2,1)S(1)} %collective-permute-done.27.refs_5_), channel_id=1, source_target_pairs={{0,8},{8,16},{16,24},{24,28},{28,20},{20,12},{12,4},{4,0},{1,9},{9... | collective-permute-start | bytes 737288 | tf_op jit(solution)/shard_map/ppermute | solution.py:299
  64.6 18.2 %collective-permute-start.33 = (bf16[80,3072]{1,0:T(8,128)(2,1)S(1)}, bf16[80,3072]{1,0:T(8,128)(2,1)S(1)}, u32[]{:S(2)}, u32[]{:S(2)}) collective-permute-start(bf16[80,3072]{1,0:T(8,128)(2,1)S(1)} %collective-permute-done.29.refs_2_), channel_id=1, source_target_pairs={{0,8},{8,16},{16,24},{24,28},{28,20},{20,12},{12,4},{4,0},{1,9},{9... | collective-permute-start | bytes 1474568 | tf_op jit(solution)/shard_map/ppermute | solution.py:299
  65.3 17.6 %collective-permute-start.34 = (bf16[80,3072]{1,0:T(8,128)(2,1)S(1)}, bf16[80,3072]{1,0:T(8,128)(2,1)S(1)}, u32[]{:S(2)}, u32[]{:S(2)}) collective-permute-start(bf16[80,3072]{1,0:T(8,128)(2,1)S(1)} %collective-permute-done.30.refs_10_), channel_id=1, source_target_pairs={{8,0},{16,8},{24,16},{28,24},{20,28},{12,20},{4,12},{0,4},{9,1},{1... | collective-permute-start | bytes 1474568 | tf_op jit(solution)/shard_map/ppermute | solution.py:299
  73.4 9.5 %collective-permute-start.32 = (bf16[80,1536]{1,0:T(8,128)(2,1)S(1)}, bf16[80,1536]{1,0:T(8,128)(2,1)S(1)}, u32[]{:S(2)}, u32[]{:S(2)}) collective-permute-start(bf16[80,1536]{1,0:T(8,128)(2,1)S(1)} %collective-permute-done.28.refs_5_), channel_id=1, source_target_pairs={{8,0},{16,8},{24,16},{28,24},{20,28},{12,20},{4,12},{0,4},{9,1},{1... | collective-permute-start | bytes 737288 | tf_op jit(solution)/shard_map/ppermute | solution.py:299
  82.9 16.9 %collective-permute-start.40 = (bf16[80,3072]{1,0:T(8,128)(2,1)S(1)}, bf16[80,3072]{1,0:T(8,128)(2,1)S(1)}, u32[]{:S(2)}, u32[]{:S(2)}) collective-permute-start(bf16[80,3072]{1,0:T(8,128)(2,1)S(1)} %collective-permute-done.33.refs_3_), channel_id=1, source_target_pairs={{0,8},{8,16},{16,24},{24,28},{28,20},{20,12},{12,4},{4,0},{1,9},{9... | collective-permute-start | bytes 1474568 | tf_op jit(solution)/shard_map/ppermute | solution.py:299
  83.6 16.1 %collective-permute-start.41 = (bf16[80,3072]{1,0:T(8,128)(2,1)S(1)}, bf16[80,3072]{1,0:T(8,128)(2,1)S(1)}, u32[]{:S(2)}, u32[]{:S(2)}) collective-permute-start(bf16[80,3072]{1,0:T(8,128)(2,1)S(1)} %collective-permute-done.34.refs_11_), channel_id=1, source_target_pairs={{8,0},{16,8},{24,16},{28,24},{20,28},{12,20},{4,12},{0,4},{9,1},{1... | collective-permute-start | bytes 1474568 | tf_op jit(solution)/shard_map/ppermute | solution.py:299
  84.9 14.6 %collective-permute-start.38 = (bf16[80,1536]{1,0:T(8,128)(2,1)S(1)}, bf16[80,1536]{1,0:T(8,128)(2,1)S(1)}, u32[]{:S(2)}, u32[]{:S(2)}) collective-permute-start(bf16[80,1536]{1,0:T(8,128)(2,1)S(1)} %collective-permute-done.31.refs_6_), channel_id=1, source_target_pairs={{0,8},{8,16},{16,24},{24,28},{28,20},{20,12},{12,4},{4,0},{1,9},{9... | collective-permute-start | bytes 737288 | tf_op jit(solution)/shard_map/ppermute | solution.py:299
  85.7 46.4 %copy-start.7 = (bf16[256,2304]{1,0:T(8,128)(2,1)}, bf16[256,2304]{1,0:T(8,128)(2,1)S(1)}, u32[]{:S(2)}) copy-start(bf16[256,2304]{1,0:T(8,128)(2,1)S(1)} %collective-permute-done.35.refs_1_) | copy-start | bytes 3538948
  85.7 14.1 %collective-permute-start.39 = (bf16[80,1536]{1,0:T(8,128)(2,1)S(1)}, bf16[80,1536]{1,0:T(8,128)(2,1)S(1)}, u32[]{:S(2)}, u32[]{:S(2)}) collective-permute-start(bf16[80,1536]{1,0:T(8,128)(2,1)S(1)} %collective-permute-done.32.refs_6_), channel_id=1, source_target_pairs={{8,0},{16,8},{24,16},{28,24},{20,28},{12,20},{4,12},{0,4},{9,1},{1... | collective-permute-start | bytes 737288 | tf_op jit(solution)/shard_map/ppermute | solution.py:299
  86.9 45.2 %copy-start.8 = (bf16[256,2304]{1,0:T(8,128)(2,1)}, bf16[256,2304]{1,0:T(8,128)(2,1)S(1)}, u32[]{:S(2)}) copy-start(bf16[256,2304]{1,0:T(8,128)(2,1)S(1)} %collective-permute-done.37.refs_3_) | copy-start | bytes 3538948
  99.7 11.1 %collective-permute-start.42 = (bf16[80,3072]{1,0:T(8,128)(2,1)S(1)}, bf16[80,3072]{1,0:T(8,128)(2,1)S(1)}, u32[]{:S(2)}, u32[]{:S(2)}) collective-permute-start(bf16[80,3072]{1,0:T(8,128)(2,1)S(1)} %collective-permute-done.40.refs_4_), channel_id=1, source_target_pairs={{0,8},{8,16},{16,24},{24,28},{28,20},{20,12},{12,4},{4,0},{1,9},{9... | collective-permute-start | bytes 1474568 | tf_op jit(solution)/shard_map/ppermute | solution.py:299
  101.0 10.1 %collective-permute-start.43 = (bf16[80,3072]{1,0:T(8,128)(2,1)S(1)}, bf16[80,3072]{1,0:T(8,128)(2,1)S(1)}, u32[]{:S(2)}, u32[]{:S(2)}) collective-permute-start(bf16[80,3072]{1,0:T(8,128)(2,1)S(1)} %collective-permute-done.41.refs_12_), channel_id=1, source_target_pairs={{8,0},{16,8},{24,16},{28,24},{20,28},{12,20},{4,12},{0,4},{9,1},{1... | collective-permute-start | bytes 1474568 | tf_op jit(solution)/shard_map/ppermute | solution.py:299
  111.0 11.1 %collective-permute-start.44 = (bf16[80,3072]{1,0:T(8,128)(2,1)S(1)}, bf16[80,3072]{1,0:T(8,128)(2,1)S(1)}, u32[]{:S(2)}, u32[]{:S(2)}) collective-permute-start(bf16[80,3072]{1,0:T(8,128)(2,1)S(1)} %collective-permute-done.42.refs_5_), channel_id=1, source_target_pairs={{0,8},{8,16},{16,24},{24,28},{28,20},{20,12},{12,4},{4,0},{1,9},{9... | collective-permute-start | bytes 1474568 | tf_op jit(solution)/shard_map/ppermute | solution.py:299
  112.1 10.1 %collective-permute-start.45 = (bf16[80,3072]{1,0:T(8,128)(2,1)S(1)}, bf16[80,3072]{1,0:T(8,128)(2,1)S(1)}, u32[]{:S(2)}, u32[]{:S(2)}) collective-permute-start(bf16[80,3072]{1,0:T(8,128)(2,1)S(1)} %collective-permute-done.43.refs_13_), channel_id=1, source_target_pairs={{8,0},{16,8},{24,16},{28,24},{20,28},{12,20},{4,12},{0,4},{9,1},{1... | collective-permute-start | bytes 1474568 | tf_op jit(solution)/shard_map/ppermute | solution.py:299
  122.1 9.0 %collective-permute-start.46 = (bf16[80,3072]{1,0:T(8,128)(2,1)S(1)}, bf16[80,3072]{1,0:T(8,128)(2,1)S(1)}, u32[]{:S(2)}, u32[]{:S(2)}) collective-permute-start(bf16[80,3072]{1,0:T(8,128)(2,1)S(1)} %collective-permute-done.44.refs_6_), channel_id=1, source_target_pairs={{0,8},{8,16},{16,24},{24,28},{28,20},{20,12},{12,4},{4,0},{1,9},{9... | collective-permute-start | bytes 1474568 | tf_op jit(solution)/shard_map/ppermute | solution.py:299
  123.2 8.9 %collective-permute-start.47 = (bf16[80,3072]{1,0:T(8,128)(2,1)S(1)}, bf16[80,3072]{1,0:T(8,128)(2,1)S(1)}, u32[]{:S(2)}, u32[]{:S(2)}) collective-permute-start(bf16[80,3072]{1,0:T(8,128)(2,1)S(1)} %collective-permute-done.45.refs_14_), channel_id=1, source_target_pairs={{8,0},{16,8},{24,16},{28,24},{20,28},{12,20},{4,12},{0,4},{9,1},{1... | collective-permute-start | bytes 1474568 | tf_op jit(solution)/shard_map/ppermute | solution.py:299
